TPU v7x, 32 devices: a whole 2x2x4 slice. The times are simulated.
32 devices in a mesh: chan: 2 (over x), tm: 16 (over z, y, core).
Axes of the slice: x: 2, y: 2, z: 4, core: 2. Of those that a mesh axis runs over, the one named last changes fastest.
Arguments:
- voltages: bfloat16 [8, 2, 128, 32768], P(None, None, 'chan', 'tm'), may hold values from -100 to 100
- prototype: float32 [64], replicated, may hold values from -5 to 5
- forget: float32 [8], P('chan'), may hold values from 0.5 to 16
Outputs:
- whitened: bfloat16 [8, 256, 32768], P('chan', None, 'tm')
All inputs are finite; a program needn't handle non-finite values.
Results may differ from a plain program's by a relative error of at most 0.0071.
Values may be sent and summed in bfloat16 or wider, within the bound.
A program may use at most 128 MiB of HBM per device.

v0:
```python
import math

import jax
import jax.numpy as jnp
from jax import lax
from jax.sharding import PartitionSpec as P


def passed_along(value, axis, steps):
    count = lax.axis_size(axis)
    leading, last = (max(0, -steps), min(count, count - steps))
    return lax.ppermute(value, axis, [(source, source + steps) for source in range(leading, last)])


def carried_in(value, axis, join, neutral):
    count, mine = (lax.axis_size(axis), lax.axis_index(axis))
    pieces = jax.tree.map(lambda part: lax.all_gather(part, axis), value)
    total = jax.tree.map(
        lambda part, zero: jnp.full_like(part, 0) + jnp.asarray(zero, part.dtype), value, neutral
    )

    def hop(position, total):
        longer = join(total, jax.tree.map(lambda part: part[position], pieces))
        return jax.tree.map(lambda new, old: jnp.where(position < mine, new, old), longer, total)

    return lax.fori_loop(0, count - 1, hop, total)


def coefficient_table(prototype, tap_count, filter_branches):
    shaped = prototype.reshape(tap_count, filter_branches)
    steps_p = jnp.arange(filter_branches, dtype=jnp.float32)
    phase = 2.0 * math.pi / filter_branches * (steps_p[:, None] * steps_p[None, :])
    cosine = jnp.cos(phase)
    sine = jnp.sin(phase)
    pattern = jnp.stack([jnp.stack([cosine, -sine], -1), jnp.stack([sine, cosine], -1)], axis=1)
    return (shaped[:, :, None, None, None] * pattern[None]).astype(jnp.bfloat16)


def combine_stats(earlier, later):
    gram_e, count_e, retain_e = earlier
    gram_l, count_l, retain_l = later
    return (
        gram_e * retain_l[:, None, None] + gram_l,
        count_e * retain_l + count_l,
        retain_e * retain_l,
    )


def per_device(voltages, prototype, forget):
    filter_branches = voltages.shape[0]
    local_antenna_count = voltages.shape[2]
    frame_rows = voltages.shape[3]
    tap_count = prototype.shape[0] // filter_branches
    coef_table = coefficient_table(prototype, tap_count, filter_branches)
    tail_rows = passed_along(voltages[..., frame_rows - (tap_count - 1) :], "tm", 1)
    extended = jnp.concatenate([tail_rows, voltages], axis=3)
    branch_sum = jnp.zeros((filter_branches, local_antenna_count, 2, frame_rows), jnp.float32)
    for tap_idx in range(tap_count):
        branch_sum = branch_sum + jnp.einsum(
            "pcaf,pckq->kaqf",
            extended[..., tap_idx : tap_idx + frame_rows],
            coef_table[tap_idx],
            preferred_element_type=jnp.float32,
        )
    spectrum_rows = branch_sum.reshape(filter_branches, local_antenna_count * 2, frame_rows).astype(
        jnp.bfloat16
    )
    turned = lax.all_to_all(spectrum_rows, "chan", split_axis=0, concat_axis=1, tiled=True)
    channels_per_device = turned.shape[0]
    col_count = turned.shape[1]
    gram_now = jnp.einsum("cif,cjf->cij", turned, turned, preferred_element_type=jnp.float32)
    retain = jnp.exp(-forget / lax.axis_size("tm"))
    row_count = jnp.full((channels_per_device,), float(frame_rows), jnp.float32)
    zero_count = jnp.zeros((channels_per_device,), jnp.float32)
    unit_retain = jnp.ones((channels_per_device,), jnp.float32)
    prior_gram, prior_count, unused_retain = carried_in(
        (gram_now, row_count, retain),
        "tm",
        combine_stats,
        (jnp.zeros_like(gram_now), zero_count, unit_retain),
    )
    moment = retain[:, None, None] * prior_gram + gram_now
    weight_sum = retain * prior_count + jnp.float32(frame_rows)
    factor_low = jnp.linalg.cholesky(moment / weight_sum[:, None, None])
    identity_m = jnp.broadcast_to(jnp.eye(col_count, dtype=jnp.float32), factor_low.shape)
    inverse = lax.linalg.triangular_solve(factor_low, identity_m, left_side=True, lower=True)
    whitened = jnp.einsum(
        "cij,cjf->cif", inverse, turned.astype(jnp.float32), precision=lax.Precision.HIGHEST
    )
    return whitened.astype(jnp.bfloat16)


def solution(mesh):
    placed = (P(None, None, "chan", "tm"), P(), P("chan"))
    return jax.shard_map(
        per_device, mesh=mesh, in_specs=placed, out_specs=P("chan", None, "tm"), check_vma=False
    )
```

profile of v0, /device:TPU:25, one launch (start us, length us, event | category | flops | bytes accessed | tf_op | source)
XLA Modules:
  0.0 518.4 jit_solution(17428512622586569670)
XLA Ops:
  6.5 4.5 copy.45
  13.2 3.7 collective-permute-start
  17.2 10.4 %fusion.35 = f32[8,2,64,2048,1]{3,0,4,2,1:T(8,128)} fusion(bf16[8,8,2,8,2]{1,3,2,4,0:T(8,128)(2,1)S(1)} %multiply_convert_fusion, bf16[8,2,64,2048]{3,2,1,0:T(8,128)(2,1)} %param.5), kind=kOutput, calls=%fused_computation.48 | convolution fusion | flops 67108864 | bytes 12591104 | tf_op jit(solution)/shard_map/pcaf,pckq->kaqf/dot_general | solution.py:59
  27.6 4.2 fusion.12
  31.8 4.0 fusion.16
  35.8 4.0 fusion.20
  39.8 4.0 fusion.24
  43.8 4.0 fusion.4
  47.9 4.0 fusion.8
  51.8 21.3 %fusion.37 = bf16[8,64,2,2048]{3,0,1,2:T(8,128)(2,1)} fusion(f32[8,2,64,2048,1]{3,0,4,2,1:T(8,128)} %fusion.35, bf16[8,2,64,2048]{3,0,1,2:T(8,128)(2,1)S(1)} %copy-done.1, bf16[8,2,64,7]{3,0,1,2:T(8,128)(2,1)S(1)} %collective-permute-done, f32[8,2,64,2048,1]{3,0,4,2,1:T(8,128)} %fusion.4, f32[8,2,64,2048,1]{3,0,4,2,1:T(8,128)} %fusion.24, ...), kind=kOutput, calls=%fused_computation.51 | convolution fusion | flops 92274688 | bytes 67379200 | tf_op jit(solution)/shard_map/pcaf,pckq->kaqf/dot_general | solution.py:59
  73.1 2.5 copy.48
  75.6 2.3 copy.49
  77.9 49.6 %all_to_all.18 = bf16[8,128,2048]{2,1,0:T(8,128)(2,1)S(1)} all-to-all(bf16[8,128,2048]{2,1,0:T(8,128)(2,1)S(1)} %copy.49), channel_id=1, replica_groups=mesh['chan'=2,'tm'=16] {'chan'}, dimensions={0} | all-to-all | bytes 8388608 | tf_op jit(solution)/shard_map/all_to_all | solution.py:68
  130.1 2.2 fusion.73
  133.8 23.5 %all-reduce.1 = f32[64]{0:T(128)S(1)} all-reduce(f32[64]{0:T(128)S(1)} %get-tuple-element.189), channel_id=2, replica_groups=mesh['chan'=2,'tm'=16] {'tm'}, use_global_device_ids=true, to_apply=%add.1 | all-reduce | flops 64 | bytes 512
  159.1 97.6 %all-gather.4.cloned.1.call-done = f32[64,256,256]{2,1,0:T(8,128)} async-done(((f32[4,256,256]{2,1,0:T(8,128)}), f32[64,256,256]{2,1,0:T(8,128)}) %all-gather.4.cloned.1.call-update) | async-done | bytes 16777232 | tf_op jit(solution)/shard_map/all_gather | solution.py:17
  256.7 24.2 %while.18 = (s32[]{:T(128)}, f32[4,256,256]{2,1,0:T(8,128)S(1)}, f32[4]{0:T(128)S(1)}, s32[]{:T(128)}, f32[16,4]{1,0:T(8,128)S(1)}, /*index=5*/f32[16,4,256,256]{3,2,1,0:T(8,128)}, s32[]{:T(128)}, s32[]{:T(128)}) while((s32[]{:T(128)}, f32[4,256,256]{2,1,0:T(8,128)S(1)}, f32[4]{0:T(128)S(1)}, s32[]{:T(128)}, ...), condition=%wide.region_1.2_spmd.clone, body=%wide.region_0.1_spmd.clone.sunk | while | flops 1048596 | bytes 3145923 | solution.py:26
  282.0 46.9 %custom-call.16 = f32[4,128,128]{2,1,0:T(8,128)S(1)} custom-call(f32[4,128,128]{2,1,0:T(8,128)S(1)} %cholesky.119), custom_call_target="Cholesky" | custom-call | tf_op jit(solution)/shard_map/jit(cholesky)/cholesky | solution.py:84
  329.0 39.3 %custom-call.17 = f32[4,1,128,128]{2,3,1,0:T(8,128)S(1)} custom-call(f32[4,1,128,128]{3,2,1,0:T(8,128)S(1)} %select_bitcast_fusion), custom_call_target="InvertDiagBlocksLowerTriangular" | custom-call | tf_op jit(solution)/shard_map/jit(cholesky)/cholesky | solution.py:84
  369.4 47.1 %custom-call.18 = f32[4,128,128]{2,1,0:T(8,128)S(1)} custom-call(f32[4,128,128]{2,1,0:T(8,128)S(1)} %convolution_subtract_fusion.1), custom_call_target="Cholesky" | custom-call | tf_op jit(solution)/shard_map/jit(cholesky)/cholesky | solution.py:84
  417.1 5.3 %while.17 = (s32[]{:T(128)}, f32[4,256,256]{2,1,0:T(8,128)S(1)}, s32[2,2]{1,0:T(2,128)S(1)}, f32[2,4,128,128]{3,2,0,1:T(8,128)}, s32[]{:T(128)}) while((s32[]{:T(128)}, f32[4,256,256]{2,1,0:T(8,128)S(1)}, s32[2,2]{1,0:T(2,128)S(1)}, f32[2,4,128,128]{3,2,0,1:T(8,128)}, s32[]{:T(128)}) %tuple.59), condition=%wide.while_cond, body=%wide.while_body.sunk | while | flops 2 | bytes 525921 | solution.py:86
  420.4 2.1 bitcast_dynamic-update-slice_fusion.2
  422.4 79.4 %custom-call.19 = f32[4,2,128,128]{2,3,1,0:T(8,128)S(1)} custom-call(f32[4,2,128,128]{3,2,1,0:T(8,128)} %bitcast.194), custom_call_target="InvertDiagBlocksLowerTriangular" | custom-call | tf_op jit(solution)/shard_map/triangular_solve | solution.py:86
  503.7 7.4 %convolution_convert_fusion = bf16[4,256,2048]{2,1,0:T(8,128)(2,1)} fusion(bf16[4,256,2048]{2,1,0:T(8,128)(2,1)} %bitcast.190, f32[4,128,256]{2,1,0:T(8,128)S(1)} %fusion.51, f32[4,128,256]{2,1,0:T(8,128)S(1)} %fusion.52), kind=kOutput, calls=%fused_computation.50 | convolution fusion | flops 6444810240 | bytes 9437184 | tf_op jit(solution)/shard_map/cij,cjf->cif/dot_general | solution.py:87
  (92 shorter events, 39.1 us)
Async XLA Ops:
  6.5 10.6 %copy-start.3 = (f32[64]{0:T(128)S(1)}, f32[64]{0:T(128)}, u32[]{:S(2)}) copy-start(f32[64]{0:T(128)} %param.6) | copy-start | bytes 772
  6.5 250.2 %all-gather.4.cloned.1.call-start = ((), (), s32[]{:S(2)}) async-start(), calls=%async_computation.1 | async-start | bytes 17825792 | tf_op jit(solution)/shard_map/all_gather | solution.py:17
  11.0 2.0 copy-start
  13.2 14.4 %collective-permute-start = (bf16[8,2,64,7]{3,0,1,2:T(8,128)(2,1)S(1)}, bf16[8,2,64,7]{3,0,1,2:T(8,128)(2,1)S(1)}, u32[]{:S(2)}, u32[]{:S(2)}) collective-permute-start(bf16[8,2,64,7]{3,0,1,2:T(8,128)(2,1)S(1)} %slice.122), channel_id=1, source_target_pairs={{0,1},{1,2},{2,3},{3,4},{4,5},{5,6},{6,7},{7,8},{8,9},{9,10},{10,1... | collective-permute-start | bytes 43016 | tf_op jit(solution)/shard_map/ppermute | solution.py:12
  17.2 10.4 %copy-start.1 = (bf16[8,2,64,2048]{3,0,1,2:T(8,128)(2,1)S(1)}, bf16[8,2,64,2048]{3,0,1,2:T(8,128)(2,1)}, u32[]{:S(2)}) copy-start(bf16[8,2,64,2048]{3,0,1,2:T(8,128)(2,1)} %copy-done) | copy-start | bytes 12582916
  128.2 1.9 copy-start.2
  130.1 2.3 copy-start.5
  130.1 3.6 copy-start.4
Sparse Core Ops, SparseCore 0:
  132.5 124.1 all-gather.3
where the time goes:
time: 529 us; the launch traced here: 518 us
  other arithmetic  238 us (45%)
  waiting for transfers between devices  97.6 us (18%)
  blocking collectives  73.2 us (14%)
  matrix products  68.5 us (13%)
  local copies, waits for them, and re-layouts  22.5 us (4%)
  between operations  14.8 us (3%)
    another operation x10, other arithmetic, per_device(): factor_low = jnp.linalg.cholesky(moment / weight_sum[:, None, None])  134 us
    all_gather x1, waiting for transfers between devices, carried_in(): pieces = jax.tree.map(lambda part: lax.all_gather(part, axis), value)  97.6 us
    another operation x4, other arithmetic, per_device(): lax.linalg.triangular_solve(factor_low, identity_m, left_side=True, lower...  79.6 us
    dot_general x8, matrix products, per_device(): jnp.einsum('pcaf,pckq->kaqf', extended[..., tap_idx:tap_idx + frame_rows]...  55.9 us
    all_to_all x1, blocking collectives, per_device(): lax.all_to_all(spectrum_rows, 'chan', split_axis=0, concat_axis=1, tiled=...  49.6 us
    select_n x30, other arithmetic, hop(): jnp.where(position < mine, new, old)  23.8 us
    unnamed x1, blocking collectives  23.5 us
  transfers between devices with their start and end apart: 2, of which 1 were waited for; matrix products, arithmetic and copies ran while one was open for 3% of the time, Pallas kernels for 0%

commit v1 on v0

--- a/solution.py
+++ b/solution.py
@@ -3,7 +3,13 @@
 import jax
 import jax.numpy as jnp
 from jax import lax
+from jax.experimental import pallas as pl
+from jax.experimental.pallas import tpu as pltpu
 from jax.sharding import PartitionSpec as P
+
+
+GROUP = 8
+BASE = 128
 
 
 def passed_along(value, axis, steps):
@@ -81,13 +87,133 @@
     )
     moment = retain[:, None, None] * prior_gram + gram_now
     weight_sum = retain * prior_count + jnp.float32(frame_rows)
-    factor_low = jnp.linalg.cholesky(moment / weight_sum[:, None, None])
-    identity_m = jnp.broadcast_to(jnp.eye(col_count, dtype=jnp.float32), factor_low.shape)
-    inverse = lax.linalg.triangular_solve(factor_low, identity_m, left_side=True, lower=True)
-    whitened = jnp.einsum(
-        "cij,cjf->cif", inverse, turned.astype(jnp.float32), precision=lax.Precision.HIGHEST
-    )
-    return whitened.astype(jnp.bfloat16)
+    scaled = moment / weight_sum[:, None, None]
+    half = col_count // 2
+    blocks = jnp.stack(
+        [scaled[:, :half, :half], scaled[:, half:, :half], scaled[:, half:, half:]], axis=1
+    )
+    return whitened_by(blocks, turned)
+
+
+def split3(x):
+    high = x.astype(jnp.bfloat16)
+    rest = x - high.astype(jnp.float32)
+    mid = rest.astype(jnp.bfloat16)
+    low = (rest - mid.astype(jnp.float32)).astype(jnp.bfloat16)
+    return high, mid, low
+
+
+def exact_dot(a, b, dims):
+    return lax.dot_general(
+        a, b, (dims, ((), ())), precision=lax.Precision.HIGHEST, preferred_element_type=jnp.float32
+    )
+
+
+def eliminate(work, done, channels):
+    lane = lax.broadcasted_iota(jnp.int32, (GROUP, BASE), 1)
+    row = lax.broadcasted_iota(jnp.int32, (GROUP, BASE), 0)
+
+    def group_step(group, _):
+        first = pl.multiple_of(group * GROUP, GROUP)
+        trailing = lane < BASE - first
+        panels, columns, scales = [], [], []
+        for c in range(channels):
+            panel = work[c, pl.ds(first, GROUP), :]
+            columns.append(
+                [jnp.broadcast_to(panel[:, q : q + 1], (GROUP, BASE)) for q in range(GROUP)]
+            )
+            panels.append(jnp.where(lane < GROUP, (lane == row).astype(jnp.float32), panel))
+            scales.append(jnp.zeros((GROUP, BASE), jnp.float32))
+        for p in range(GROUP):
+            for c in range(channels):
+                column = columns[c]
+                pivot = jnp.broadcast_to(column[p][p : p + 1, :], (GROUP, BASE))
+                inverse = 1.0 / pivot
+                scales[c] = jnp.where(row == p, inverse, scales[c])
+                if p + 1 < GROUP:
+                    factor = jnp.where(row > p, column[p] * inverse, 0.0)
+                    for q in range(p + 1, GROUP):
+                        column[q] = column[q] - factor * column[q][p : p + 1, :]
+                    panels[c] = panels[c] - factor * panels[c][p : p + 1, :]
+        for c in range(channels):
+            panel = panels[c]
+            scaled = panel * scales[c]
+            final = jnp.where(trailing & (lane >= GROUP), 0.0, panel) * jnp.sqrt(scales[c])
+            done[c, pl.ds(first, GROUP), :] = pltpu.roll(final, first, 1)
+            left = pltpu.roll(jnp.where(trailing & (lane >= GROUP), panel, 0.0), first, 1)
+            lh, lm, ll = split3(left)
+            rh, rm, rl = split3(scaled)
+            lefts = jnp.concatenate([lh, lh, lh, lm, lm, ll], 0)
+            rights = jnp.concatenate([rh, rm, rl, rh, rm, rh], 0)
+            update = lax.dot_general(
+                lefts, rights, (((0,), (0,)), ((), ())), preferred_element_type=jnp.float32
+            )
+            wide = lax.broadcasted_iota(jnp.int32, (BASE, BASE), 1)
+            kept = jnp.where(wide < GROUP, 0.0, work[c])
+            work[c] = pltpu.roll(kept - update, BASE - GROUP, 1)
+        return 0
+
+    lax.fori_loop(0, BASE // GROUP, group_step, 0)
+
+
+def whiten_kernel(moment_ref, x_ref, out_ref, work, done, low21, high, low):
+    channels = moment_ref.shape[0]
+    step = pl.program_id(0)
+
+    @pl.when(step == 0)
+    def _():
+        for c in range(channels):
+            work[c] = moment_ref[c, 0]
+        eliminate(work, done, channels)
+        for c in range(channels):
+            inverse = done[c]
+            factor = exact_dot(moment_ref[c, 1], inverse, ((1,), (1,)))
+            work[c] = moment_ref[c, 2] - exact_dot(factor, factor, ((1,), (1,)))
+            low21[c] = exact_dot(factor, inverse, ((1,), (0,)))
+            first = inverse.astype(jnp.bfloat16)
+            high[c, :BASE, :BASE] = first
+            low[c, :BASE, :BASE] = (inverse - first.astype(jnp.float32)).astype(jnp.bfloat16)
+            high[c, :BASE, BASE:] = jnp.zeros((BASE, BASE), jnp.bfloat16)
+            low[c, :BASE, BASE:] = jnp.zeros((BASE, BASE), jnp.bfloat16)
+        eliminate(work, done, channels)
+        for c in range(channels):
+            inverse = done[c]
+            corner = -exact_dot(inverse, low21[c], ((1,), (0,)))
+            for at, part in ((0, corner), (BASE, inverse)):
+                first = part.astype(jnp.bfloat16)
+                high[c, BASE:, at : at + BASE] = first
+                low[c, BASE:, at : at + BASE] = (part - first.astype(jnp.float32)).astype(
+                    jnp.bfloat16
+                )
+
+    x = x_ref[0]
+    total = jnp.dot(high[step], x, preferred_element_type=jnp.float32)
+    total += jnp.dot(low[step], x, preferred_element_type=jnp.float32)
+    out_ref[0] = total.astype(jnp.bfloat16)
+
+
+def whitened_by(moment, spectra):
+    channels, rows, frames = spectra.shape
+    square = (channels, BASE, BASE)
+    return pl.pallas_call(
+        whiten_kernel,
+        grid=(channels,),
+        out_shape=jax.ShapeDtypeStruct(spectra.shape, jnp.bfloat16),
+        in_specs=[
+            pl.BlockSpec((channels, 3, BASE, BASE), lambda c: (0, 0, 0, 0)),
+            pl.BlockSpec((1, rows, frames), lambda c: (c, 0, 0)),
+        ],
+        out_specs=pl.BlockSpec((1, rows, frames), lambda c: (c, 0, 0)),
+        scratch_shapes=[
+            pltpu.VMEM(square, jnp.float32),
+            pltpu.VMEM(square, jnp.float32),
+            pltpu.VMEM(square, jnp.float32),
+            pltpu.VMEM((channels, rows, rows), jnp.bfloat16),
+            pltpu.VMEM((channels, rows, rows), jnp.bfloat16),
+        ],
+        compiler_params=pltpu.CompilerParams(vmem_limit_bytes=40 << 20),
+        name="whiten",
+    )(moment, spectra)
 
 
 def solution(mesh):

time: 529 us -> 320 us (0.60); the launches traced: 518 us -> 315 us
  other arithmetic: 238 us -> 24.4 us
  Pallas kernels: 0 us -> 25.4 us
  matrix products: 68.5 us -> 58.1 us
  local copies, waits for them, and re-layouts: 22.5 us -> 16.7 us
    another operation x14 -> x1, other arithmetic: 213 us -> 0.05 us  [per_device(): jnp.stack([scaled[:, :half, :half], scaled[:, half:, :half], scaled[:, ha...]
    pallas_call x0 -> x1, Pallas kernels: none -> 25.4 us  [whitened_by(): pl.pallas_call(whiten_kernel, grid=(channels,), out_shape=jax.ShapeDtypeS...]
    dot_general x1 -> x0, matrix products: 7.44 us -> none  [per_device(): jnp.einsum('cij,cjf->cif', inverse, turned.astype(jnp.float32), precision...]
    another operation x10 -> x1, local copies, waits for them, and re-layouts: 5.49 us -> 0.07 us  [per_device(): jnp.stack([scaled[:, :half, :half], scaled[:, half:, :half], scaled[:, ha...]
    unnamed x15 -> x19, local copies, waits for them, and re-layouts: 9.1 us -> 10.9 us
  transfers between devices with their start and end apart: 2 -> 2, of which waited for: 1 -> 1; matrix products, arithmetic and copies ran while one was open for 3% -> 4% of each run, Pallas kernels for 0% -> 0%
where the time goes in v1:
time: 320 us; the launch traced here: 315 us
  waiting for transfers between devices  99.6 us (31%)
  blocking collectives  72.9 us (23%)
  matrix products  58.1 us (18%)
  Pallas kernels  25.4 us (8%)
  other arithmetic  24.4 us (8%)
  local copies, waits for them, and re-layouts  16.7 us (5%)
  between operations  14.2 us (4%)
  starting transfers between devices  3.71 us (1%)
    all_gather x1, waiting for transfers between devices, carried_in(): pieces = jax.tree.map(lambda part: lax.all_gather(part, axis), value)  99.6 us
    dot_general x8, matrix products, per_device(): jnp.einsum('pcaf,pckq->kaqf', extended[..., tap_idx:tap_idx + frame_rows]...  55.8 us
    all_to_all x1, blocking collectives, per_device(): lax.all_to_all(spectrum_rows, 'chan', split_axis=0, concat_axis=1, tiled=...  49.6 us
    pallas_call x1, Pallas kernels, whitened_by(): pl.pallas_call(whiten_kernel, grid=(channels,), out_shape=jax.ShapeDtypeS...  25.4 us
    select_n x30, other arithmetic, hop(): jnp.where(position < mine, new, old)  23.9 us
    unnamed x1, blocking collectives  23.3 us
    unnamed x19, local copies, waits for them, and re-layouts  10.9 us
  transfers between devices with their start and end apart: 2, of which 1 were waited for; matrix products, arithmetic and copies ran while one was open for 4% of the time, Pallas kernels for 0%

profile of v1, /device:TPU:25, one launch (start us, length us, event | category | flops | bytes accessed | tf_op | source)
XLA Modules:
  0.0 315.5 jit_solution(10553822712730514556)
XLA Ops:
  6.5 4.5 %copy.20 = bf16[8,2,64,2048]{3,0,1,2:T(8,128)(2,1)S(1)} copy(bf16[8,2,64,2048]{3,2,1,0:T(8,128)(2,1)} %param.5) | data formatting | bytes 8388608 | tf_op args[0]
  11.0 2.0 copy-done.2
  13.2 3.7 %collective-permute-start = (bf16[8,2,64,7]{3,0,1,2:T(8,128)(2,1)S(1)}, bf16[8,2,64,7]{3,0,1,2:T(8,128)(2,1)S(1)}, u32[]{:S(2)}, u32[]{:S(2)}) collective-permute-start(bf16[8,2,64,7]{3,0,1,2:T(8,128)(2,1)S(1)} %slice.77), channel_id=1, source_target_pairs={{0,1},{1,2},{2,3},{3,4},{4,5},{5,6},{6,7},{7,8},{8,9},{9,10},{10,1... | collective-permute-start | bytes 43016 | tf_op jit(solution)/shard_map/ppermute | solution.py:18
  17.2 10.4 %fusion.35 = f32[8,2,64,2048,1]{3,0,4,2,1:T(8,128)} fusion(bf16[8,8,2,8,2]{1,3,2,4,0:T(8,128)(2,1)S(1)} %multiply_convert_fusion, bf16[8,2,64,2048]{3,2,1,0:T(8,128)(2,1)} %param.5), kind=kOutput, calls=%fused_computation.46 | convolution fusion | flops 67108864 | bytes 12591104 | tf_op jit(solution)/shard_map/pcaf,pckq->kaqf/dot_general | solution.py:65
  27.6 4.0 %fusion.12 = f32[8,2,64,2048,1]{3,0,4,2,1:T(8,128)} fusion(bf16[8,2,64,7]{3,0,1,2:T(8,128)(2,1)S(1)} %collective-permute-done, bf16[8,2,64,2048]{3,0,1,2:T(8,128)(2,1)S(1)} %copy-done.3, bf16[8,8,2,8,2]{1,3,2,4,0:T(8,128)(2,1)S(1)} %multiply_convert_fusion), kind=kOutput, calls=%fused_computation.27 | convolution fusion | flops 75497472 | bytes 12853248 | tf_op jit(solution)/shard_map/pcaf,pckq->kaqf/dot_general | solution.py:65
  31.6 4.0 %fusion.16 = f32[8,2,64,2048,1]{3,0,4,2,1:T(8,128)} fusion(bf16[8,2,64,7]{3,0,1,2:T(8,128)(2,1)S(1)} %collective-permute-done, bf16[8,2,64,2048]{3,0,1,2:T(8,128)(2,1)S(1)} %copy-done.3, bf16[8,8,2,8,2]{1,3,2,4,0:T(8,128)(2,1)S(1)} %multiply_convert_fusion), kind=kOutput, calls=%fused_computation.30 | convolution fusion | flops 75497472 | bytes 12853248 | tf_op jit(solution)/shard_map/pcaf,pckq->kaqf/dot_general | solution.py:65
  35.7 4.0 %fusion.20 = f32[8,2,64,2048,1]{3,0,4,2,1:T(8,128)} fusion(bf16[8,2,64,7]{3,0,1,2:T(8,128)(2,1)S(1)} %collective-permute-done, bf16[8,2,64,2048]{3,0,1,2:T(8,128)(2,1)S(1)} %copy-done.3, bf16[8,8,2,8,2]{1,3,2,4,0:T(8,128)(2,1)S(1)} %multiply_convert_fusion), kind=kOutput, calls=%fused_computation.33 | convolution fusion | flops 75497472 | bytes 12853248 | tf_op jit(solution)/shard_map/pcaf,pckq->kaqf/dot_general | solution.py:65
  39.7 4.0 %fusion.24 = f32[8,2,64,2048,1]{3,0,4,2,1:T(8,128)} fusion(bf16[8,2,64,7]{3,0,1,2:T(8,128)(2,1)S(1)} %collective-permute-done, bf16[8,2,64,2048]{3,0,1,2:T(8,128)(2,1)S(1)} %copy-done.3, bf16[8,8,2,8,2]{1,3,2,4,0:T(8,128)(2,1)S(1)} %multiply_convert_fusion), kind=kOutput, calls=%fused_computation.36 | convolution fusion | flops 75497472 | bytes 12853248 | tf_op jit(solution)/shard_map/pcaf,pckq->kaqf/dot_general | solution.py:65
  43.7 4.0 %fusion.4 = f32[8,2,64,2048,1]{3,0,4,2,1:T(8,128)} fusion(bf16[8,2,64,7]{3,0,1,2:T(8,128)(2,1)S(1)} %collective-permute-done, bf16[8,2,64,2048]{3,0,1,2:T(8,128)(2,1)S(1)} %copy-done.3, bf16[8,8,2,8,2]{1,3,2,4,0:T(8,128)(2,1)S(1)} %multiply_convert_fusion), kind=kOutput, calls=%fused_computation.21 | convolution fusion | flops 75497472 | bytes 12853248 | tf_op jit(solution)/shard_map/pcaf,pckq->kaqf/dot_general | solution.py:65
  47.7 4.0 %fusion.8 = f32[8,2,64,2048,1]{3,0,4,2,1:T(8,128)} fusion(bf16[8,2,64,7]{3,0,1,2:T(8,128)(2,1)S(1)} %collective-permute-done, bf16[8,2,64,2048]{3,0,1,2:T(8,128)(2,1)S(1)} %copy-done.3, bf16[8,8,2,8,2]{1,3,2,4,0:T(8,128)(2,1)S(1)} %multiply_convert_fusion), kind=kOutput, calls=%fused_computation.24 | convolution fusion | flops 75497472 | bytes 12853248 | tf_op jit(solution)/shard_map/pcaf,pckq->kaqf/dot_general | solution.py:65
  51.7 21.3 %fusion.37 = bf16[8,64,2,2048]{3,0,1,2:T(8,128)(2,1)} fusion(f32[8,2,64,2048,1]{3,0,4,2,1:T(8,128)} %fusion.35, bf16[8,2,64,2048]{3,0,1,2:T(8,128)(2,1)S(1)} %copy-done.3, bf16[8,2,64,7]{3,0,1,2:T(8,128)(2,1)S(1)} %collective-permute-done, f32[8,2,64,2048,1]{3,0,4,2,1:T(8,128)} %fusion.4, f32[8,2,64,2048,1]{3,0,4,2,1:T(8,128)} %fusion.24, ...), kind=kOutput, calls=%fused_computation.48 | convolution fusion | flops 92274688 | bytes 67379200 | tf_op jit(solution)/shard_map/pcaf,pckq->kaqf/dot_general | solution.py:65
  73.0 2.5 copy.23
  75.5 2.3 copy.24
  77.8 49.6 %all_to_all.18 = bf16[8,128,2048]{2,1,0:T(8,128)(2,1)S(1)} all-to-all(bf16[8,128,2048]{2,1,0:T(8,128)(2,1)S(1)} %copy.24), channel_id=1, replica_groups=mesh['chan'=2,'tm'=16] {'chan'}, dimensions={0} | all-to-all | bytes 8388608 | tf_op jit(solution)/shard_map/all_to_all | solution.py:74
  128.1 2.3 fusion.58
  130.4 2.0 copy-done
  133.8 23.3 %all-reduce = f32[64]{0:T(128)S(1)} all-reduce(f32[64]{0:T(128)S(1)} %get-tuple-element.169), channel_id=2, replica_groups=mesh['chan'=2,'tm'=16] {'tm'}, use_global_device_ids=true, to_apply=%add | all-reduce | flops 64 | bytes 512
  157.1 99.6 %all-gather.4.cloned.1.call-done = f32[64,256,256]{2,1,0:T(8,128)} async-done(((f32[4,256,256]{2,1,0:T(8,128)}), f32[64,256,256]{2,1,0:T(8,128)}) %all-gather.4.cloned.1.call-update) | async-done | bytes 16777232 | tf_op jit(solution)/shard_map/all_gather | solution.py:23
  256.7 24.3 %while.16 = (s32[]{:T(128)}, f32[4,256,256]{2,1,0:T(8,128)S(1)}, f32[4]{0:T(128)S(1)}, s32[]{:T(128)}, f32[16,4]{1,0:T(8,128)S(1)}, /*index=5*/f32[16,4,256,256]{3,2,1,0:T(8,128)}, s32[]{:T(128)}, s32[]{:T(128)}) while((s32[]{:T(128)}, f32[4,256,256]{2,1,0:T(8,128)S(1)}, f32[4]{0:T(128)S(1)}, s32[]{:T(128)}, ...), condition=%wide.region_1.2_spmd.clone, body=%wide.region_0.1_spmd.clone.sunk | while | flops 1048596 | bytes 3145923 | solution.py:32
  256.7 1.6 fusion.62
  264.9 1.6 fusion.62
  266.5 1.6 fusion.62
  281.4 1.8 copy-done.1
  283.2 25.4 %whiten.1 = bf16[4,256,2048]{2,1,0:T(8,128)(2,1)} custom-call(f32[4,3,128,128]{3,2,1,0:T(8,128)S(1)} %pad_maximum_fusion.1.moment_ref, bf16[4,256,2048]{2,1,0:T(8,128)(2,1)S(1)} %bitcast.163), custom_call_target="tpu_custom_call" | custom-call | tf_op jit(solution)/shard_map/whiten/pallas_call | solution.py:198
  (62 shorter events, 21.3 us)
Async XLA Ops:
  6.5 10.6 %copy-start.5 = (f32[64]{0:T(128)S(1)}, f32[64]{0:T(128)}, u32[]{:S(2)}) copy-start(f32[64]{0:T(128)} %param.6) | copy-start | bytes 772
  6.5 250.2 %all-gather.4.cloned.1.call-start = ((), (), s32[]{:S(2)}) async-start(), calls=%async_computation.1 | async-start | bytes 17825792 | tf_op jit(solution)/shard_map/all_gather | solution.py:23
  11.0 2.0 copy-start.2
  13.2 14.4 %collective-permute-start = (bf16[8,2,64,7]{3,0,1,2:T(8,128)(2,1)S(1)}, bf16[8,2,64,7]{3,0,1,2:T(8,128)(2,1)S(1)}, u32[]{:S(2)}, u32[]{:S(2)}) collective-permute-start(bf16[8,2,64,7]{3,0,1,2:T(8,128)(2,1)S(1)} %slice.77), channel_id=1, source_target_pairs={{0,1},{1,2},{2,3},{3,4},{4,5},{5,6},{6,7},{7,8},{8,9},{9,10},{10,1... | collective-permute-start | bytes 43016 | tf_op jit(solution)/shard_map/ppermute | solution.py:18
  17.2 10.4 %copy-start.3 = (bf16[8,2,64,2048]{3,0,1,2:T(8,128)(2,1)S(1)}, bf16[8,2,64,2048]{3,0,1,2:T(8,128)(2,1)}, u32[]{:S(2)}) copy-start(bf16[8,2,64,2048]{3,0,1,2:T(8,128)(2,1)} %copy-done.2) | copy-start | bytes 12582916
  128.1 4.4 %copy-start.7 = (u32[32]{0:T(128)S(1)}, u32[32]{0:T(128)}, u32[]{:S(2)}) copy-start(u32[32]{0:T(128)} %constant.42) | copy-start | bytes 388
  128.1 5.6 %copy-start.6 = (f32[4]{0:T(128)S(1)}, f32[4]{0:T(128)}, u32[]{:S(2)}) copy-start(f32[4]{0:T(128)} %param.7) | copy-start | bytes 52
  130.4 2.0 copy-start
  256.7 24.3 %copy-start.4 = (f32[4,256,256]{2,1,0:T(8,128)S(1)}, f32[4,256,256]{2,1,0:T(8,128)}, u32[]{:S(2)}) copy-start(f32[4,256,256]{2,1,0:T(8,128)} %fusion.58) | copy-start | bytes 3145732
  281.0 2.2 copy-start.1
Sparse Core Ops, SparseCore 0:
  132.5 124.1 all-gather.3

commit v2 on v1

--- a/solution.py
+++ b/solution.py
@@ -1,3 +1,4 @@
+import functools
 import math
 
 import jax
@@ -7,92 +8,8 @@
 from jax.experimental.pallas import tpu as pltpu
 from jax.sharding import PartitionSpec as P
 
-
 GROUP = 8
 BASE = 128
-
-
-def passed_along(value, axis, steps):
-    count = lax.axis_size(axis)
-    leading, last = (max(0, -steps), min(count, count - steps))
-    return lax.ppermute(value, axis, [(source, source + steps) for source in range(leading, last)])
-
-
-def carried_in(value, axis, join, neutral):
-    count, mine = (lax.axis_size(axis), lax.axis_index(axis))
-    pieces = jax.tree.map(lambda part: lax.all_gather(part, axis), value)
-    total = jax.tree.map(
-        lambda part, zero: jnp.full_like(part, 0) + jnp.asarray(zero, part.dtype), value, neutral
-    )
-
-    def hop(position, total):
-        longer = join(total, jax.tree.map(lambda part: part[position], pieces))
-        return jax.tree.map(lambda new, old: jnp.where(position < mine, new, old), longer, total)
-
-    return lax.fori_loop(0, count - 1, hop, total)
-
-
-def coefficient_table(prototype, tap_count, filter_branches):
-    shaped = prototype.reshape(tap_count, filter_branches)
-    steps_p = jnp.arange(filter_branches, dtype=jnp.float32)
-    phase = 2.0 * math.pi / filter_branches * (steps_p[:, None] * steps_p[None, :])
-    cosine = jnp.cos(phase)
-    sine = jnp.sin(phase)
-    pattern = jnp.stack([jnp.stack([cosine, -sine], -1), jnp.stack([sine, cosine], -1)], axis=1)
-    return (shaped[:, :, None, None, None] * pattern[None]).astype(jnp.bfloat16)
-
-
-def combine_stats(earlier, later):
-    gram_e, count_e, retain_e = earlier
-    gram_l, count_l, retain_l = later
-    return (
-        gram_e * retain_l[:, None, None] + gram_l,
-        count_e * retain_l + count_l,
-        retain_e * retain_l,
-    )
-
-
-def per_device(voltages, prototype, forget):
-    filter_branches = voltages.shape[0]
-    local_antenna_count = voltages.shape[2]
-    frame_rows = voltages.shape[3]
-    tap_count = prototype.shape[0] // filter_branches
-    coef_table = coefficient_table(prototype, tap_count, filter_branches)
-    tail_rows = passed_along(voltages[..., frame_rows - (tap_count - 1) :], "tm", 1)
-    extended = jnp.concatenate([tail_rows, voltages], axis=3)
-    branch_sum = jnp.zeros((filter_branches, local_antenna_count, 2, frame_rows), jnp.float32)
-    for tap_idx in range(tap_count):
-        branch_sum = branch_sum + jnp.einsum(
-            "pcaf,pckq->kaqf",
-            extended[..., tap_idx : tap_idx + frame_rows],
-            coef_table[tap_idx],
-            preferred_element_type=jnp.float32,
-        )
-    spectrum_rows = branch_sum.reshape(filter_branches, local_antenna_count * 2, frame_rows).astype(
-        jnp.bfloat16
-    )
-    turned = lax.all_to_all(spectrum_rows, "chan", split_axis=0, concat_axis=1, tiled=True)
-    channels_per_device = turned.shape[0]
-    col_count = turned.shape[1]
-    gram_now = jnp.einsum("cif,cjf->cij", turned, turned, preferred_element_type=jnp.float32)
-    retain = jnp.exp(-forget / lax.axis_size("tm"))
-    row_count = jnp.full((channels_per_device,), float(frame_rows), jnp.float32)
-    zero_count = jnp.zeros((channels_per_device,), jnp.float32)
-    unit_retain = jnp.ones((channels_per_device,), jnp.float32)
-    prior_gram, prior_count, unused_retain = carried_in(
-        (gram_now, row_count, retain),
-        "tm",
-        combine_stats,
-        (jnp.zeros_like(gram_now), zero_count, unit_retain),
-    )
-    moment = retain[:, None, None] * prior_gram + gram_now
-    weight_sum = retain * prior_count + jnp.float32(frame_rows)
-    scaled = moment / weight_sum[:, None, None]
-    half = col_count // 2
-    blocks = jnp.stack(
-        [scaled[:, :half, :half], scaled[:, half:, :half], scaled[:, half:, half:]], axis=1
-    )
-    return whitened_by(blocks, turned)
 
 
 def split3(x):
@@ -216,6 +133,311 @@
     )(moment, spectra)
 
 
+PLANE = 4
+PIECE = 16
+HALO = 128
+TILE = 512
+
+
+def digits(shape, axis, unit, count):
+    return (lax.broadcasted_iota(jnp.int32, shape, axis) // unit) % count
+
+
+def turn_kernel(
+    taps, chan_count, tm_count,
+    volts, coef, retain, inverse_weight,
+    spectra, moment,
+    extended, table, outgoing, gram, plane_in, chain_in, chain_out, plane_out,
+    load_sem, halo_send, halo_recv, turn_send, turn_recv,
+    spread_send, spread_recv, chain_send, chain_recv, back_send, back_recv,
+):
+    inputs, antennas, frames = volts.shape
+    channels = spectra.shape[0]
+    pieces = antennas // PIECE
+    piece_rows = 2 * PIECE
+    quarter = moment.shape[1] // PLANE
+    chan, tm = lax.axis_index("chan"), lax.axis_index("tm")
+    plane, spot = tm // PLANE, tm % PLANE
+    plane_count = tm_count // PLANE
+
+    def remote(src, dst, send, recv, chan_to, tm_to):
+        return pltpu.make_async_remote_copy(
+            src_ref=src, dst_ref=dst, send_sem=send, recv_sem=recv,
+            device_id=(chan_to, tm_to), device_id_type=pl.DeviceIdType.MESH,
+        )
+
+    def mate(step):
+        return plane * PLANE + (spot + step) % PLANE
+
+    loads = []
+    for g in range(pieces):
+        rows = pl.ds(g * PIECE, PIECE)
+        loads.append(
+            pltpu.make_async_copy(
+                volts.at[:, rows, :], extended.at[:, rows, pl.ds(HALO, frames)], load_sem.at[g]
+            )
+        )
+        loads[-1].start()
+
+    barrier = pltpu.get_barrier_semaphore()
+
+    def greet(chan_to, tm_to):
+        pl.semaphore_signal(
+            barrier, inc=1, device_id=(chan_to, tm_to), device_id_type=pl.DeviceIdType.MESH
+        )
+
+    for s in range(1, chan_count):
+        greet((chan + s) % chan_count, tm)
+    for m in range(1, PLANE):
+        greet(chan, mate(m))
+    above, below = plane + 1 < plane_count, plane > 0
+    peers = chan_count - 1 + PLANE - 1
+    for step, reached in (
+        (PLANE, above), (-PLANE, below), (1, above & (spot == PLANE - 1)), (-1, below & (spot == 0))
+    ):
+        peers = peers + jnp.where(reached, 1, 0)
+
+        @pl.when(reached)
+        def _():
+            greet(chan, tm + step)
+
+    rows, columns = table.shape
+    kinds, terms = coef.shape
+    pick_row = digits((rows, kinds), 0, piece_rows, rows // piece_rows) * 2 + digits((rows, kinds), 0, 1, 2)
+    pick_row = pick_row == lax.broadcasted_iota(jnp.int32, (rows, kinds), 1)
+    pick_column = digits((terms, columns), 1, PIECE, terms)
+    pick_column = pick_column == lax.broadcasted_iota(jnp.int32, (terms, columns), 0)
+    spread = jnp.dot(
+        pick_row.astype(jnp.float32).astype(jnp.bfloat16), coef[...], preferred_element_type=jnp.float32
+    ).astype(jnp.bfloat16)
+    spread = jnp.dot(
+        spread, pick_column.astype(jnp.float32).astype(jnp.bfloat16), preferred_element_type=jnp.float32
+    )
+    own = digits((rows, columns), 0, 2, PIECE) == digits((rows, columns), 1, 1, PIECE)
+    table[...] = jnp.where(own, spread, 0.0).astype(jnp.bfloat16)
+
+    pl.semaphore_wait(barrier, peers)
+
+    tail = remote(
+        volts.at[:, :, pl.ds(frames - HALO, HALO)], extended.at[:, :, pl.ds(0, HALO)],
+        halo_send, halo_recv, chan, tm + 1,
+    )
+
+    @pl.when(tm + 1 < tm_count)
+    def _():
+        tail.start()
+
+    @pl.when(tm == 0)
+    def _():
+        extended[:, :, :HALO] = jnp.zeros((inputs, antennas, HALO), jnp.bfloat16)
+
+    @pl.when(tm > 0)
+    def _():
+        tail.wait_recv()
+
+    base = chan * (2 * antennas)
+    turns = {}
+
+    def send_rows(s, c, g, start, count):
+        turns[s, c, g] = remote(
+            outgoing.at[s - 1, c, pl.ds(start, count), :],
+            spectra.at[c, pl.ds(pl.multiple_of(base + start, piece_rows), count), :],
+            turn_send.at[s - 1, c, g], turn_recv.at[s - 1, c, g],
+            (chan + s) % chan_count, tm,
+        )
+        turns[s, c, g].start()
+
+    for g in range(pieces):
+        loads[g].wait()
+
+        def tile(t, _):
+            first = pl.multiple_of(t * TILE, TILE)
+            block = extended[:, g * PIECE : (g + 1) * PIECE, pl.ds(first, TILE + HALO)]
+            block = block.reshape(inputs * PIECE, TILE + HALO)
+            shifted = [
+                (pltpu.roll(block, taps - 1 - j, 1) if j < taps - 1 else block)[:, HALO:]
+                for j in range(taps)
+            ]
+            result = jnp.dot(
+                table[...], jnp.concatenate(shifted, 0), preferred_element_type=jnp.float32
+            ).astype(jnp.bfloat16)
+            for s in range(chan_count):
+                for c in range(channels):
+                    at = (s * channels + c) * piece_rows
+                    part = result[at : at + piece_rows]
+                    if s == 0:
+                        start = pl.multiple_of(base + g * piece_rows, piece_rows)
+                        spectra[c, pl.ds(start, piece_rows), pl.ds(first, TILE)] = part
+                    else:
+                        outgoing[s - 1, c, g * piece_rows : (g + 1) * piece_rows, pl.ds(first, TILE)] = part
+            return 0
+
+        lax.fori_loop(0, frames // TILE, tile, 0)
+        for s in range(1, chan_count):
+            send_rows(s, 0, g, g * piece_rows, piece_rows)
+    for c in range(1, channels):
+        for s in range(1, chan_count):
+            send_rows(s, c, 0, 0, pieces * piece_rows)
+
+    spreads, chains, backs = {}, {}, {}
+    half = 2 * antennas * chan_count // 2
+
+    def part_of(index):
+        return pl.ds(pl.multiple_of(index * quarter, 8), quarter)
+
+    def own_block(c):
+        for key, copy in turns.items():
+            if key[1] == c:
+                copy.wait_recv()
+        x = spectra[c]
+        product = lax.dot_general(
+            x, x, (((1,), (1,)), ((), ())), preferred_element_type=jnp.float32
+        )
+        gram[c, :half] = product[:half, :half]
+        gram[c, half : 2 * half] = product[half:, :half]
+        gram[c, 2 * half :] = product[half:, half:]
+        for m in range(1, PLANE):
+            spreads[c, m] = remote(
+                gram.at[c, part_of((spot + m) % PLANE), :], plane_in.at[c, spot],
+                spread_send.at[c, m - 1], spread_recv.at[c, m - 1], chan, mate(m),
+            )
+            spreads[c, m].start()
+        plane_in[c, spot] = gram[c, part_of(spot), :]
+
+    def carry(c):
+        for m in range(1, PLANE):
+            spreads[c, m].wait_recv()
+        keep = retain[c]
+        total = plane_in[c, 0]
+        for i in range(1, PLANE):
+            total = total * keep + plane_in[c, i]
+        chains[c] = remote(
+            chain_out.at[c], chain_in.at[c], chain_send.at[c], chain_recv.at[c], chan, tm + PLANE
+        )
+
+        @pl.when(plane == 0)
+        def _():
+            chain_in[c] = jnp.zeros_like(total)
+
+        @pl.when(plane > 0)
+        def _():
+            chains[c].wait_recv()
+
+        running = chain_in[c]
+        square = keep * keep
+        chain_out[c] = running * (square * square) + total
+
+        @pl.when(plane + 1 < plane_count)
+        def _():
+            chains[c].start()
+
+        for i in range(PLANE):
+            running = running * keep + plane_in[c, i]
+            plane_out[c, i] = running * inverse_weight[c, i]
+        for m in range(1, PLANE):
+            backs[c, m] = remote(
+                plane_out.at[c, (spot + m) % PLANE], moment.at[c, part_of(spot), :],
+                back_send.at[c, m - 1], back_recv.at[c, m - 1], chan, mate(m),
+            )
+            backs[c, m].start()
+        moment[c, part_of(spot), :] = plane_out[c, spot]
+
+    for c in range(channels):
+        own_block(c)
+        if c > 0:
+            carry(c - 1)
+    carry(channels - 1)
+
+    for copy in backs.values():
+        copy.wait()
+    for copy in spreads.values():
+        copy.wait_send()
+    for copy in turns.values():
+        copy.wait_send()
+
+    @pl.when(plane + 1 < plane_count)
+    def _():
+        for copy in chains.values():
+            copy.wait_send()
+
+    @pl.when(tm + 1 < tm_count)
+    def _():
+        tail.wait_send()
+
+
+def turned_and_carried(volts, coef, retain, inverse_weight, taps):
+    inputs, antennas, frames = volts.shape
+    channels = retain.shape[0]
+    chan_count, tm_count = lax.axis_size("chan"), lax.axis_size("tm")
+    columns = 2 * antennas * chan_count
+    half = columns // 2
+    quarter = 3 * half // PLANE
+    rows = coef.shape[0] * PIECE
+    pieces = antennas // PIECE
+    dma = pltpu.SemaphoreType.DMA
+    turn_shape = (chan_count - 1, channels, pieces)
+    plane_shape = (channels, PLANE - 1)
+    return pl.pallas_call(
+        functools.partial(turn_kernel, taps, chan_count, tm_count),
+        out_shape=(
+            jax.ShapeDtypeStruct((channels, columns, frames), jnp.bfloat16),
+            jax.ShapeDtypeStruct((channels, 3 * half, half), jnp.float32),
+        ),
+        in_specs=[
+            pl.BlockSpec(memory_space=pl.ANY),
+            pl.BlockSpec(memory_space=pltpu.VMEM),
+            pl.BlockSpec(memory_space=pltpu.SMEM),
+            pl.BlockSpec(memory_space=pltpu.SMEM),
+        ],
+        out_specs=(pl.BlockSpec(memory_space=pltpu.VMEM), pl.BlockSpec(memory_space=pltpu.VMEM)),
+        scratch_shapes=[
+            pltpu.VMEM((inputs, antennas, HALO + frames), jnp.bfloat16),
+            pltpu.VMEM((rows, taps * inputs * PIECE), jnp.bfloat16),
+            pltpu.VMEM((chan_count - 1, channels, 2 * antennas, frames), jnp.bfloat16),
+            pltpu.VMEM((channels, 3 * half, half), jnp.float32),
+            pltpu.VMEM((channels, PLANE, quarter, half), jnp.float32),
+            pltpu.VMEM((channels, quarter, half), jnp.float32),
+            pltpu.VMEM((channels, quarter, half), jnp.float32),
+            pltpu.VMEM((channels, PLANE, quarter, half), jnp.float32),
+            dma((pieces,)), dma, dma, dma(turn_shape), dma(turn_shape),
+            dma(plane_shape), dma(plane_shape), dma((channels,)), dma((channels,)),
+            dma(plane_shape), dma(plane_shape),
+        ],
+        compiler_params=pltpu.CompilerParams(
+            collective_id=0, has_side_effects=True, vmem_limit_bytes=40 << 20
+        ),
+        name="turn",
+    )(volts, coef, retain, inverse_weight)
+
+
+def coefficient_rows(prototype, tap_count, branches, first):
+    shaped = prototype.reshape(tap_count, branches)
+    steps_p = jnp.arange(branches, dtype=jnp.float32)
+    steps_k = ((jnp.arange(branches) + first) % branches).astype(jnp.float32)
+    phase = 2.0 * math.pi / branches * (steps_k[:, None] * steps_p[None, :])
+    cosine, sine = jnp.cos(phase), jnp.sin(phase)
+    pattern = jnp.stack([jnp.stack([cosine, sine], -1), jnp.stack([-sine, cosine], -1)], axis=1)
+    table = shaped[None, None, :, :, None] * pattern[:, :, None, :, :]
+    return table.astype(jnp.bfloat16).reshape(2 * branches, tap_count * branches * 2)
+
+
+def per_device(voltages, prototype, forget):
+    branches, parts, antennas, frames = voltages.shape
+    taps = prototype.shape[0] // branches
+    channels = forget.shape[0]
+    tm_count = lax.axis_size("tm")
+    coef = coefficient_rows(prototype, taps, branches, lax.axis_index("chan") * channels)
+    rate = -forget / tm_count
+    ages = jnp.arange(tm_count)
+    spots = lax.axis_index("tm") // PLANE * PLANE + jnp.arange(PLANE)
+    held = jnp.where(ages <= spots[:, None], 1.0, 0.0)
+    powers = jnp.exp(rate[:, None] * ages.astype(jnp.float32))
+    weight = frames * jnp.sum(powers[:, None, :] * held[None], -1)
+    volts = voltages.reshape(branches * parts, antennas, frames)
+    spectra, moment = turned_and_carried(volts, coef, jnp.exp(rate), 1.0 / weight, taps)
+    return whitened_by(moment.reshape(channels, 3, BASE, BASE), spectra)
+
+
 def solution(mesh):
     placed = (P(None, None, "chan", "tm"), P(), P("chan"))
     return jax.shard_map(

time: 320 us -> 107 us (0.33); the launches traced: 315 us -> 106 us
  waiting for transfers between devices: 99.6 us -> 0 us
  Pallas kernels: 25.4 us -> 102 us
  blocking collectives: 72.9 us -> 0 us
  matrix products: 58.1 us -> 0 us
  other arithmetic: 24.4 us -> 0.98 us
  between operations: 14.2 us -> 0.07 us
  local copies, waits for them, and re-layouts: 16.7 us -> 3.61 us
  starting transfers between devices: 3.71 us -> 0 us
    all_gather x1 -> x0, waiting for transfers between devices: 99.6 us -> none  [carried_in(): pieces = jax.tree.map(lambda part: lax.all_gather(part, axis), value)]
    pallas_call x0 -> x1, Pallas kernels: none -> 76.1 us  [turned_and_carried(): pl.pallas_call(functools.partial(turn_kernel, taps, chan_count, tm_count)...]
    dot_general x9 -> x0, matrix products: 58.1 us -> none  [the longest x8 55.8 us: per_device(): jnp.einsum('pcaf,pckq->kaqf', extended[..., tap_idx:tap_idx + frame_rows]...]
    all_to_all x1 -> x0, blocking collectives: 49.6 us -> none  [per_device(): lax.all_to_all(spectrum_rows, 'chan', split_axis=0, concat_axis=1, tiled=...]
    select_n x30 -> x0, other arithmetic: 23.9 us -> none  [hop(): jnp.where(position < mine, new, old)]
    unnamed x1 -> x0, blocking collectives: 23.3 us -> none
    unnamed x19 -> x2, local copies, waits for them, and re-layouts: 10.9 us -> 2.18 us
    convert_element_type x2 -> x0, local copies, waits for them, and re-layouts: 4.79 us -> none  [per_device(): branch_sum.reshape(filter_branches, local_antenna_count * 2, frame_rows)]
  transfers between devices with their start and end apart: 2 -> 0, of which waited for: 1 -> 0; matrix products, arithmetic and copies ran while one was open for 4% -> 0% of each run, Pallas kernels for 0% -> 0%
where the time goes in v2:
time: 107 us; the launch traced here: 106 us
  Pallas kernels  102 us (95%)
  local copies, waits for them, and re-layouts  3.61 us (3%)
    pallas_call x1, Pallas kernels, turned_and_carried(): pl.pallas_call(functools.partial(turn_kernel, taps, chan_count, tm_count)...  76.1 us
    pallas_call x1, Pallas kernels, whitened_by(): pl.pallas_call(whiten_kernel, grid=(channels,), out_shape=jax.ShapeDtypeS...  25.4 us
    unnamed x2, local copies, waits for them, and re-layouts  2.18 us

profile of v2, /device:TPU:25, one launch (start us, length us, event | category | flops | bytes accessed | tf_op | source)
XLA Modules:
  0.0 106.2 jit_solution(13479874192161582333)
XLA Ops:
  0.0 0.7 negate_multiply_fusion
  0.7 0.1 multiply_exponential_fusion
  0.8 0.1 multiply_reduce_fusion
  0.9 0.7 mul.110
  1.6 0.1 fusion
  1.8 0.1 mul.111
  1.8 0.1 mul.112
  2.0 0.2 copy.6
  2.2 0.3 mul.121
  2.5 0.0 copy-start
  2.5 2.2 %copy-done = bf16[8,2,64,2048]{3,2,1,0:T(8,128)(2,1)S(1)} copy-done((bf16[8,2,64,2048]{3,2,1,0:T(8,128)(2,1)S(1)}, bf16[8,2,64,2048]{3,2,1,0:T(8,128)(2,1)}, u32[]{:S(2)}) %copy-start) | copy-done | bytes 4194328
  4.7 76.1 %turn.1 = (bf16[4,256,2048]{2,1,0:T(8,128)(2,1)S(1)}, f32[4,384,128]{2,1,0:T(8,128)S(1)}) custom-call(bf16[16,64,2048]{2,1,0:T(8,128)(2,1)S(1)} %bitcast.8, bf16[16,128]{1,0:T(8,128)(2,1)S(1)} %multiply_convert_fusion.coef, f32[4]{0:T(128)S(1)} %get-tuple-element.12.retain, f32[4,4]{1,0:T(4,128)S(1)} %multiply_divide_fusion.inverse_weight), custom_call_target="tpu_custom_call" | custom-call | tf_op jit(solution)/shard_map/turn/pallas_call | solution.py:380
  80.7 25.4 %whiten.1 = bf16[4,256,2048]{2,1,0:T(8,128)(2,1)} custom-call(f32[4,3,128,128]{3,2,1,0:T(8,128)S(1)} %bitcast.9, bf16[4,256,2048]{2,1,0:T(8,128)(2,1)S(1)} %get-tuple-element.8.x_ref), custom_call_target="tpu_custom_call" | custom-call | tf_op jit(solution)/shard_map/whiten/pallas_call | solution.py:115
  (8 shorter events, 0.1 us)
Async XLA Ops:
  2.5 2.2 %copy-start = (bf16[8,2,64,2048]{3,2,1,0:T(8,128)(2,1)S(1)}, bf16[8,2,64,2048]{3,2,1,0:T(8,128)(2,1)}, u32[]{:S(2)}) copy-start(bf16[8,2,64,2048]{3,2,1,0:T(8,128)(2,1)} %param.3) | copy-start | bytes 12582916

commit v3 on v2

--- a/solution.py
+++ b/solution.py
@@ -3,12 +3,14 @@
 
 import jax
 import jax.numpy as jnp
+import numpy as np
 from jax import lax
 from jax.experimental import pallas as pl
 from jax.experimental.pallas import tpu as pltpu
 from jax.sharding import PartitionSpec as P
 
-GROUP = 8
+GROUP = 16
+SUB = 8
 BASE = 128
 
 
@@ -29,37 +31,51 @@
 def eliminate(work, done, channels):
     lane = lax.broadcasted_iota(jnp.int32, (GROUP, BASE), 1)
     row = lax.broadcasted_iota(jnp.int32, (GROUP, BASE), 0)
+    below = lax.broadcasted_iota(jnp.int32, (SUB, BASE), 0)
+    subs = GROUP // SUB
 
     def group_step(group, _):
         first = pl.multiple_of(group * GROUP, GROUP)
-        trailing = lane < BASE - first
+        trailing = (lane < BASE - first) & (lane >= GROUP)
         panels, columns, scales = [], [], []
-        for c in range(channels):
+        for c in channels:
             panel = work[c, pl.ds(first, GROUP), :]
-            columns.append(
-                [jnp.broadcast_to(panel[:, q : q + 1], (GROUP, BASE)) for q in range(GROUP)]
-            )
-            panels.append(jnp.where(lane < GROUP, (lane == row).astype(jnp.float32), panel))
-            scales.append(jnp.zeros((GROUP, BASE), jnp.float32))
+            columns.append([
+                [
+                    jnp.broadcast_to(panel[h * SUB : (h + 1) * SUB, q : q + 1], (SUB, BASE))
+                    for h in range(subs)
+                ]
+                for q in range(GROUP)
+            ])
+            panel = jnp.where(lane < GROUP, (lane == row).astype(jnp.float32), panel)
+            panels.append([panel[h * SUB : (h + 1) * SUB] for h in range(subs)])
+            scales.append([jnp.zeros((SUB, BASE), jnp.float32) for h in range(subs)])
         for p in range(GROUP):
-            for c in range(channels):
-                column = columns[c]
-                pivot = jnp.broadcast_to(column[p][p : p + 1, :], (GROUP, BASE))
+            at, inner = p // SUB, p % SUB
+            for i in range(len(channels)):
+                column = columns[i]
+                pivot = jnp.broadcast_to(column[p][at][inner : inner + 1, :], (SUB, BASE))
                 inverse = 1.0 / pivot
-                scales[c] = jnp.where(row == p, inverse, scales[c])
-                if p + 1 < GROUP:
-                    factor = jnp.where(row > p, column[p] * inverse, 0.0)
-                    for q in range(p + 1, GROUP):
-                        column[q] = column[q] - factor * column[q][p : p + 1, :]
-                    panels[c] = panels[c] - factor * panels[c][p : p + 1, :]
-        for c in range(channels):
-            panel = panels[c]
-            scaled = panel * scales[c]
-            final = jnp.where(trailing & (lane >= GROUP), 0.0, panel) * jnp.sqrt(scales[c])
-            done[c, pl.ds(first, GROUP), :] = pltpu.roll(final, first, 1)
-            left = pltpu.roll(jnp.where(trailing & (lane >= GROUP), panel, 0.0), first, 1)
+                scales[i][at] = jnp.where(below == inner, inverse, scales[i][at])
+                for h in range(at, subs):
+                    factor = column[p][h]
+                    if h == at:
+                        factor = jnp.where(below > inner, factor, 0.0)
+                    factor = factor * inverse
+                    for part in column[p + 1 :] + [panels[i]]:
+                        if h == at:
+                            continue
+                        part[h] = part[h] - factor * part[at][inner : inner + 1, :]
+                    if h == at:
+                        own = factor
+                for part in column[p + 1 :] + [panels[i]]:
+                    part[at] = part[at] - own * part[at][inner : inner + 1, :]
+        for i, c in enumerate(channels):
+            panel = jnp.concatenate(panels[i], 0)
+            scale = jnp.concatenate(scales[i], 0)
+            left = pltpu.roll(jnp.where(trailing, panel, 0.0), first, 1)
             lh, lm, ll = split3(left)
-            rh, rm, rl = split3(scaled)
+            rh, rm, rl = split3(panel * scale)
             lefts = jnp.concatenate([lh, lh, lh, lm, lm, ll], 0)
             rights = jnp.concatenate([rh, rm, rl, rh, rm, rh], 0)
             update = lax.dot_general(
@@ -68,6 +84,8 @@
             wide = lax.broadcasted_iota(jnp.int32, (BASE, BASE), 1)
             kept = jnp.where(wide < GROUP, 0.0, work[c])
             work[c] = pltpu.roll(kept - update, BASE - GROUP, 1)
+            final = jnp.where(trailing, 0.0, panel) * jnp.sqrt(scale)
+            done[c, pl.ds(first, GROUP), :] = pltpu.roll(final, first, 1)
         return 0
 
     lax.fori_loop(0, BASE // GROUP, group_step, 0)
@@ -81,7 +99,7 @@
     def _():
         for c in range(channels):
             work[c] = moment_ref[c, 0]
-        eliminate(work, done, channels)
+        eliminate(work, done, range(channels))
         for c in range(channels):
             inverse = done[c]
             factor = exact_dot(moment_ref[c, 1], inverse, ((1,), (1,)))
@@ -92,7 +110,7 @@
             low[c, :BASE, :BASE] = (inverse - first.astype(jnp.float32)).astype(jnp.bfloat16)
             high[c, :BASE, BASE:] = jnp.zeros((BASE, BASE), jnp.bfloat16)
             low[c, :BASE, BASE:] = jnp.zeros((BASE, BASE), jnp.bfloat16)
-        eliminate(work, done, channels)
+        eliminate(work, done, range(channels))
         for c in range(channels):
             inverse = done[c]
             corner = -exact_dot(inverse, low21[c], ((1,), (0,)))
@@ -159,6 +177,7 @@
     chan, tm = lax.axis_index("chan"), lax.axis_index("tm")
     plane, spot = tm // PLANE, tm % PLANE
     plane_count = tm_count // PLANE
+    rounds = chain_out.shape[1]
 
     def remote(src, dst, send, recv, chan_to, tm_to):
         return pltpu.make_async_remote_copy(
@@ -190,11 +209,13 @@
         greet((chan + s) % chan_count, tm)
     for m in range(1, PLANE):
         greet(chan, mate(m))
-    above, below = plane + 1 < plane_count, plane > 0
     peers = chan_count - 1 + PLANE - 1
-    for step, reached in (
-        (PLANE, above), (-PLANE, below), (1, above & (spot == PLANE - 1)), (-1, below & (spot == 0))
-    ):
+    hops = [PLANE**r * d for r in range(rounds) for d in range(1, PLANE)]
+    meetings = [(PLANE * hop, plane + hop < plane_count) for hop in hops]
+    meetings += [(-PLANE * hop, plane >= hop) for hop in hops]
+    meetings.append((1, (plane + 1 < plane_count) & (spot == PLANE - 1)))
+    meetings.append((-1, (plane > 0) & (spot == 0)))
+    for step, reached in meetings:
         peers = peers + jnp.where(reached, 1, 0)
 
         @pl.when(reached)
@@ -218,23 +239,26 @@
 
     pl.semaphore_wait(barrier, peers)
 
-    tail = remote(
-        volts.at[:, :, pl.ds(frames - HALO, HALO)], extended.at[:, :, pl.ds(0, HALO)],
-        halo_send, halo_recv, chan, tm + 1,
-    )
+    tails = []
+    for g in range(pieces):
+        rows = pl.ds(g * PIECE, PIECE)
+        tails.append(
+            remote(
+                volts.at[:, rows, pl.ds(frames - HALO, HALO)], extended.at[:, rows, pl.ds(0, HALO)],
+                halo_send.at[g], halo_recv.at[g], chan, tm + 1,
+            )
+        )
 
     @pl.when(tm + 1 < tm_count)
     def _():
-        tail.start()
+        for tail in tails:
+            tail.start()
 
     @pl.when(tm == 0)
     def _():
         extended[:, :, :HALO] = jnp.zeros((inputs, antennas, HALO), jnp.bfloat16)
 
-    @pl.when(tm > 0)
-    def _():
-        tail.wait_recv()
-
+    tiles = frames // TILE
     base = chan * (2 * antennas)
     turns = {}
 
@@ -250,8 +274,12 @@
     for g in range(pieces):
         loads[g].wait()
 
-        def tile(t, _):
-            first = pl.multiple_of(t * TILE, TILE)
+        def tile(step, _):
+            @pl.when((step == tiles - 1) & (tm > 0))
+            def _():
+                tails[g].wait_recv()
+
+            first = pl.multiple_of(((step + 1) % tiles) * TILE, TILE)
             block = extended[:, g * PIECE : (g + 1) * PIECE, pl.ds(first, TILE + HALO)]
             block = block.reshape(inputs * PIECE, TILE + HALO)
             shifted = [
@@ -272,7 +300,7 @@
                         outgoing[s - 1, c, g * piece_rows : (g + 1) * piece_rows, pl.ds(first, TILE)] = part
             return 0
 
-        lax.fori_loop(0, frames // TILE, tile, 0)
+        lax.fori_loop(0, tiles, tile, 0)
         for s in range(1, chan_count):
             send_rows(s, 0, g, g * piece_rows, piece_rows)
     for c in range(1, channels):
@@ -311,26 +339,38 @@
         total = plane_in[c, 0]
         for i in range(1, PLANE):
             total = total * keep + plane_in[c, i]
-        chains[c] = remote(
-            chain_out.at[c], chain_in.at[c], chain_send.at[c], chain_recv.at[c], chan, tm + PLANE
-        )
-
-        @pl.when(plane == 0)
-        def _():
-            chain_in[c] = jnp.zeros_like(total)
-
-        @pl.when(plane > 0)
-        def _():
-            chains[c].wait_recv()
-
-        running = chain_in[c]
-        square = keep * keep
-        chain_out[c] = running * (square * square) + total
-
-        @pl.when(plane + 1 < plane_count)
-        def _():
-            chains[c].start()
-
+        reach = keep * keep
+        reach = reach * reach
+        for r in range(rounds):
+            chain_out[c, r] = total
+            span = PLANE**r
+            for d in range(1, PLANE):
+                copy = remote(
+                    chain_out.at[c, r], chain_in.at[c, r, d - 1],
+                    chain_send.at[c, r, d - 1], chain_recv.at[c, r, d - 1],
+                    chan, tm + PLANE * span * d,
+                )
+                chains[c, r, d] = copy
+
+                @pl.when(plane + span * d < plane_count)
+                def _():
+                    copy.start()
+
+                @pl.when(plane < span * d)
+                def _():
+                    chain_in[c, r, d - 1] = jnp.zeros_like(total)
+
+            earlier = jnp.zeros_like(total)
+            for d in range(PLANE - 1, 0, -1):
+                @pl.when(plane >= span * d)
+                def _():
+                    chains[c, r, d].wait_recv()
+
+                earlier = earlier * reach + chain_in[c, r, d - 1]
+            running = earlier if r == 0 else running + offset * earlier
+            total = total + reach * earlier
+            offset = reach**3 if r == 0 else offset * reach**3
+            reach = reach**4
         for i in range(PLANE):
             running = running * keep + plane_in[c, i]
             plane_out[c, i] = running * inverse_weight[c, i]
@@ -355,14 +395,15 @@
     for copy in turns.values():
         copy.wait_send()
 
-    @pl.when(plane + 1 < plane_count)
-    def _():
-        for copy in chains.values():
+    for (c, r, d), copy in chains.items():
+        @pl.when(plane + PLANE**r * d < plane_count)
+        def _():
             copy.wait_send()
 
     @pl.when(tm + 1 < tm_count)
     def _():
-        tail.wait_send()
+        for tail in tails:
+            tail.wait_send()
 
 
 def turned_and_carried(volts, coef, retain, inverse_weight, taps):
@@ -377,6 +418,10 @@
     dma = pltpu.SemaphoreType.DMA
     turn_shape = (chan_count - 1, channels, pieces)
     plane_shape = (channels, PLANE - 1)
+    rounds = 1
+    while PLANE ** (rounds + 1) < tm_count:
+        rounds += 1
+    chain_shape = (channels, rounds, PLANE - 1)
     return pl.pallas_call(
         functools.partial(turn_kernel, taps, chan_count, tm_count),
         out_shape=(
@@ -384,7 +429,7 @@
             jax.ShapeDtypeStruct((channels, 3 * half, half), jnp.float32),
         ),
         in_specs=[
-            pl.BlockSpec(memory_space=pl.ANY),
+            pl.BlockSpec(memory_space=pltpu.HBM),
             pl.BlockSpec(memory_space=pltpu.VMEM),
             pl.BlockSpec(memory_space=pltpu.SMEM),
             pl.BlockSpec(memory_space=pltpu.SMEM),
@@ -396,11 +441,11 @@
             pltpu.VMEM((chan_count - 1, channels, 2 * antennas, frames), jnp.bfloat16),
             pltpu.VMEM((channels, 3 * half, half), jnp.float32),
             pltpu.VMEM((channels, PLANE, quarter, half), jnp.float32),
-            pltpu.VMEM((channels, quarter, half), jnp.float32),
-            pltpu.VMEM((channels, quarter, half), jnp.float32),
+            pltpu.VMEM((channels, rounds, PLANE - 1, quarter, half), jnp.float32),
+            pltpu.VMEM((channels, rounds, quarter, half), jnp.float32),
             pltpu.VMEM((channels, PLANE, quarter, half), jnp.float32),
-            dma((pieces,)), dma, dma, dma(turn_shape), dma(turn_shape),
-            dma(plane_shape), dma(plane_shape), dma((channels,)), dma((channels,)),
+            dma((pieces,)), dma((pieces,)), dma((pieces,)), dma(turn_shape), dma(turn_shape),
+            dma(plane_shape), dma(plane_shape), dma(chain_shape), dma(chain_shape),
             dma(plane_shape), dma(plane_shape),
         ],
         compiler_params=pltpu.CompilerParams(
@@ -411,14 +456,13 @@
 
 
 def coefficient_rows(prototype, tap_count, branches, first):
-    shaped = prototype.reshape(tap_count, branches)
-    steps_p = jnp.arange(branches, dtype=jnp.float32)
-    steps_k = ((jnp.arange(branches) + first) % branches).astype(jnp.float32)
-    phase = 2.0 * math.pi / branches * (steps_k[:, None] * steps_p[None, :])
-    cosine, sine = jnp.cos(phase), jnp.sin(phase)
-    pattern = jnp.stack([jnp.stack([cosine, sine], -1), jnp.stack([-sine, cosine], -1)], axis=1)
-    table = shaped[None, None, :, :, None] * pattern[:, :, None, :, :]
-    return table.astype(jnp.bfloat16).reshape(2 * branches, tap_count * branches * 2)
+    steps = np.arange(branches, dtype=np.float32)
+    phase = np.float32(2.0 * math.pi / branches) * (steps[:, None] * steps[None, :])
+    cosine, sine = np.cos(phase), np.sin(phase)
+    pattern = np.stack([np.stack([cosine, sine], -1), np.stack([-sine, cosine], -1)], axis=1)
+    pattern = np.tile(pattern.reshape(2 * branches, 2 * branches), (2, tap_count))
+    pattern = lax.dynamic_slice_in_dim(jnp.asarray(pattern), 2 * first, 2 * branches, 0)
+    return (jnp.repeat(prototype, 2)[None, :] * pattern).astype(jnp.bfloat16)
 
 
 def per_device(voltages, prototype, forget):

time: 107 us -> 102 us (0.953)
  Pallas kernels: 102 us -> 96.7 us
    pallas_call x1, Pallas kernels: 25.4 us -> 22.5 us  [whitened_by(): pl.pallas_call(whiten_kernel, grid=(channels,), out_shape=jax.ShapeDtypeS...]
    pallas_call x1, Pallas kernels: 76.1 us -> 74.2 us  [turned_and_carried(): pl.pallas_call(functools.partial(turn_kernel, taps, chan_count, tm_count)...]
    mul x5 -> x1, local copies, waits for them, and re-layouts: 1.26 us -> 0.14 us  [coefficient_rows(): return (jnp.repeat(prototype, 2)[None, :] * pattern).astype(jnp.bfloat16)]
where the time goes in v3:
time: 102 us; the launch traced here: 101 us
  Pallas kernels  96.7 us (95%)
  local copies, waits for them, and re-layouts  3.07 us (3%)
  other arithmetic  1.55 us (2%)
    pallas_call x1, Pallas kernels, turned_and_carried(): pl.pallas_call(functools.partial(turn_kernel, taps, chan_count, tm_count)...  74.2 us
    pallas_call x1, Pallas kernels, whitened_by(): pl.pallas_call(whiten_kernel, grid=(channels,), out_shape=jax.ShapeDtypeS...  22.5 us
    unnamed x2, local copies, waits for them, and re-layouts  2.19 us

profile of v3, /device:TPU:25, one launch (start us, length us, event | category | flops | bytes accessed | tf_op | source)
XLA Modules:
  0.0 101.3 jit_solution(1400676048224278464)
XLA Ops:
  0.0 0.7 negate_multiply_fusion
  0.7 0.1 multiply_exponential_fusion
  0.7 0.1 multiply_reduce_fusion
  0.8 0.7 broadcast_in_dim.10
  1.6 0.1 mul.47
  1.7 0.7 multiply_convert_fusion.coef
  2.4 0.0 copy-start
  2.4 2.2 %copy-done = bf16[8,2,64,2048]{3,2,1,0:T(8,128)(2,1)S(1)} copy-done((bf16[8,2,64,2048]{3,2,1,0:T(8,128)(2,1)S(1)}, bf16[8,2,64,2048]{3,2,1,0:T(8,128)(2,1)}, u32[]{:S(2)}) %copy-start) | copy-done | bytes 4194328
  4.6 74.2 %turn.1 = (bf16[4,256,2048]{2,1,0:T(8,128)(2,1)S(1)}, f32[4,384,128]{2,1,0:T(8,128)S(1)}) custom-call(bf16[16,64,2048]{2,1,0:T(8,128)(2,1)S(1)} %bitcast.2, bf16[16,128]{1,0:T(8,128)(2,1)S(1)} %multiply_convert_fusion.coef, f32[4]{0:T(128)S(1)} %get-tuple-element.10.retain, f32[4,4]{1,0:T(4,128)S(1)} %multiply_divide_fusion.inverse_weight), custom_call_target="tpu_custom_call" | custom-call | tf_op jit(solution)/shard_map/turn/pallas_call | solution.py:425
  78.8 22.5 %whiten.1 = bf16[4,256,2048]{2,1,0:T(8,128)(2,1)} custom-call(f32[4,3,128,128]{3,2,1,0:T(8,128)S(1)} %bitcast.3, bf16[4,256,2048]{2,1,0:T(8,128)(2,1)S(1)} %get-tuple-element.8.x_ref), custom_call_target="tpu_custom_call" | custom-call | tf_op jit(solution)/shard_map/whiten/pallas_call | solution.py:133
  (3 shorter events, 0.0 us)
Async XLA Ops:
  2.4 2.2 %copy-start = (bf16[8,2,64,2048]{3,2,1,0:T(8,128)(2,1)S(1)}, bf16[8,2,64,2048]{3,2,1,0:T(8,128)(2,1)}, u32[]{:S(2)}) copy-start(bf16[8,2,64,2048]{3,2,1,0:T(8,128)(2,1)} %param.4) | copy-start | bytes 12582916

commit v4 on v3

--- a/solution.py
+++ b/solution.py
@@ -28,13 +28,15 @@
     )
 
 
-def eliminate(work, done, channels):
+def eliminate(work, done, channels, beside=None):
     lane = lax.broadcasted_iota(jnp.int32, (GROUP, BASE), 1)
     row = lax.broadcasted_iota(jnp.int32, (GROUP, BASE), 0)
     below = lax.broadcasted_iota(jnp.int32, (SUB, BASE), 0)
     subs = GROUP // SUB
 
     def group_step(group, _):
+        if beside is not None:
+            beside(group)
         first = pl.multiple_of(group * GROUP, GROUP)
         trailing = (lane < BASE - first) & (lane >= GROUP)
         panels, columns, scales = [], [], []
@@ -91,64 +93,82 @@
     lax.fori_loop(0, BASE // GROUP, group_step, 0)
 
 
-def whiten_kernel(moment_ref, x_ref, out_ref, work, done, low21, high, low):
-    channels = moment_ref.shape[0]
-    step = pl.program_id(0)
-
-    @pl.when(step == 0)
-    def _():
-        for c in range(channels):
-            work[c] = moment_ref[c, 0]
-        eliminate(work, done, range(channels))
-        for c in range(channels):
-            inverse = done[c]
-            factor = exact_dot(moment_ref[c, 1], inverse, ((1,), (1,)))
-            work[c] = moment_ref[c, 2] - exact_dot(factor, factor, ((1,), (1,)))
-            low21[c] = exact_dot(factor, inverse, ((1,), (0,)))
-            first = inverse.astype(jnp.bfloat16)
-            high[c, :BASE, :BASE] = first
-            low[c, :BASE, :BASE] = (inverse - first.astype(jnp.float32)).astype(jnp.bfloat16)
-            high[c, :BASE, BASE:] = jnp.zeros((BASE, BASE), jnp.bfloat16)
-            low[c, :BASE, BASE:] = jnp.zeros((BASE, BASE), jnp.bfloat16)
-        eliminate(work, done, range(channels))
-        for c in range(channels):
-            inverse = done[c]
-            corner = -exact_dot(inverse, low21[c], ((1,), (0,)))
-            for at, part in ((0, corner), (BASE, inverse)):
-                first = part.astype(jnp.bfloat16)
-                high[c, BASE:, at : at + BASE] = first
-                low[c, BASE:, at : at + BASE] = (part - first.astype(jnp.float32)).astype(
-                    jnp.bfloat16
-                )
-
-    x = x_ref[0]
-    total = jnp.dot(high[step], x, preferred_element_type=jnp.float32)
-    total += jnp.dot(low[step], x, preferred_element_type=jnp.float32)
-    out_ref[0] = total.astype(jnp.bfloat16)
-
-
-def whitened_by(moment, spectra):
+def invert(moment, first, count, work, done, low21, high, low, beside=(None, None)):
+    def block(i, at):
+        return moment[first + i, at * BASE : (at + 1) * BASE]
+
+    def store(i, down, across, value):
+        rows, columns = slice(down, down + BASE), slice(across, across + BASE)
+        leading = value.astype(jnp.bfloat16)
+        high[i, rows, columns] = leading
+        low[i, rows, columns] = (value - leading.astype(jnp.float32)).astype(jnp.bfloat16)
+
+    for i in range(count):
+        work[i] = block(i, 0)
+    eliminate(work, done, range(count), beside[0])
+    for i in range(count):
+        inverse = done[i]
+        factor = exact_dot(block(i, 1), inverse, ((1,), (1,)))
+        work[i] = block(i, 2) - exact_dot(factor, factor, ((1,), (1,)))
+        low21[i] = exact_dot(factor, inverse, ((1,), (0,)))
+        store(i, 0, 0, inverse)
+        store(i, 0, BASE, jnp.zeros_like(inverse))
+    eliminate(work, done, range(count), beside[1])
+    for i in range(count):
+        inverse = done[i]
+        store(i, BASE, 0, -exact_dot(inverse, low21[i], ((1,), (0,))))
+        store(i, BASE, BASE, inverse)
+
+
+def invert_scratch(count):
+    square = pltpu.VMEM((max(count, 1), BASE, BASE), jnp.float32)
+    return [square, square, square]
+
+
+def whiten_kernel(early, moment, x_ref, early_high, early_low, out_ref, work, done, low21, high, low, result, sems):
+    channels, rows, frames = x_ref.shape
+    tiles = BASE // GROUP
+    width = frames // tiles
+
+    def apply(c, upper, lower, columns):
+        x = x_ref[c, :, columns]
+        total = jnp.dot(upper, x, preferred_element_type=jnp.float32)
+        total += jnp.dot(lower, x, preferred_element_type=jnp.float32)
+        result[c, :, columns] = total.astype(jnp.bfloat16)
+
+    def tile_of(c):
+        def tile(t):
+            columns = pl.ds(pl.multiple_of(t * width, width), width)
+            apply(c, early_high[c], early_low[c], columns)
+
+        return tile
+
+    copies = [pltpu.make_async_copy(result.at[c], out_ref.at[c], sems.at[c]) for c in range(channels)]
+    beside = [tile_of(c) if c < early else None for c in range(2)]
+    invert(moment, early, channels - early, work, done, low21, high, low, beside)
+    for c in range(early):
+        copies[c].start()
+    for c in range(early, channels):
+        apply(c, high[c - early], low[c - early], slice(None))
+        copies[c].start()
+    for copy in copies:
+        copy.wait()
+
+
+def whitened_by(moment, spectra, early_high, early_low, early):
     channels, rows, frames = spectra.shape
-    square = (channels, BASE, BASE)
+    late = channels - early
+    parts = pltpu.VMEM((late, rows, rows), jnp.bfloat16)
     return pl.pallas_call(
-        whiten_kernel,
-        grid=(channels,),
+        functools.partial(whiten_kernel, early),
         out_shape=jax.ShapeDtypeStruct(spectra.shape, jnp.bfloat16),
-        in_specs=[
-            pl.BlockSpec((channels, 3, BASE, BASE), lambda c: (0, 0, 0, 0)),
-            pl.BlockSpec((1, rows, frames), lambda c: (c, 0, 0)),
-        ],
-        out_specs=pl.BlockSpec((1, rows, frames), lambda c: (c, 0, 0)),
-        scratch_shapes=[
-            pltpu.VMEM(square, jnp.float32),
-            pltpu.VMEM(square, jnp.float32),
-            pltpu.VMEM(square, jnp.float32),
-            pltpu.VMEM((channels, rows, rows), jnp.bfloat16),
-            pltpu.VMEM((channels, rows, rows), jnp.bfloat16),
-        ],
+        in_specs=[pl.BlockSpec(memory_space=pltpu.VMEM)] * 4,
+        out_specs=pl.BlockSpec(memory_space=pl.ANY),
+        scratch_shapes=invert_scratch(late)
+        + [parts, parts, pltpu.VMEM(spectra.shape, jnp.bfloat16), pltpu.SemaphoreType.DMA((channels,))],
         compiler_params=pltpu.CompilerParams(vmem_limit_bytes=40 << 20),
         name="whiten",
-    )(moment, spectra)
+    )(moment, spectra, early_high, early_low)
 
 
 PLANE = 4
@@ -162,10 +182,10 @@
 
 
 def turn_kernel(
-    taps, chan_count, tm_count,
+    taps, chan_count, tm_count, early,
     volts, coef, retain, inverse_weight,
-    spectra, moment,
-    extended, table, outgoing, gram, plane_in, chain_in, chain_out, plane_out,
+    spectra, moment, early_high, early_low,
+    work, done, low21, extended, table, outgoing, gram, plane_in, chain_in, chain_out, plane_out,
     load_sem, halo_send, halo_recv, turn_send, turn_recv,
     spread_send, spread_recv, chain_send, chain_recv, back_send, back_recv,
 ):
@@ -274,21 +294,18 @@
     for g in range(pieces):
         loads[g].wait()
 
-        def tile(step, _):
-            @pl.when((step == tiles - 1) & (tm > 0))
-            def _():
-                tails[g].wait_recv()
-
-            first = pl.multiple_of(((step + 1) % tiles) * TILE, TILE)
+        def tile(first):
             block = extended[:, g * PIECE : (g + 1) * PIECE, pl.ds(first, TILE + HALO)]
             block = block.reshape(inputs * PIECE, TILE + HALO)
             shifted = [
                 (pltpu.roll(block, taps - 1 - j, 1) if j < taps - 1 else block)[:, HALO:]
                 for j in range(taps)
             ]
-            result = jnp.dot(
+            return jnp.dot(
                 table[...], jnp.concatenate(shifted, 0), preferred_element_type=jnp.float32
             ).astype(jnp.bfloat16)
+
+        def store(first, result):
             for s in range(chan_count):
                 for c in range(channels):
                     at = (s * channels + c) * piece_rows
@@ -298,12 +315,25 @@
                         spectra[c, pl.ds(start, piece_rows), pl.ds(first, TILE)] = part
                     else:
                         outgoing[s - 1, c, g * piece_rows : (g + 1) * piece_rows, pl.ds(first, TILE)] = part
+
+        def pair(step, _):
+            @pl.when((step == tiles // 2 - 1) & (tm > 0))
+            def _():
+                tails[g].wait_recv()
+
+            places = [
+                pl.multiple_of(((step * 2 + u + 1) % tiles) * TILE, TILE) for u in range(2)
+            ]
+            results = [tile(first) for first in places]
+            for first, result in zip(places, results):
+                store(first, result)
             return 0
 
-        lax.fori_loop(0, tiles, tile, 0)
-        for s in range(1, chan_count):
-            send_rows(s, 0, g, g * piece_rows, piece_rows)
-    for c in range(1, channels):
+        lax.fori_loop(0, tiles // 2, pair, 0)
+        for c in range(max(early, 1)):
+            for s in range(1, chan_count):
+                send_rows(s, c, g, g * piece_rows, piece_rows)
+    for c in range(max(early, 1), channels):
         for s in range(1, chan_count):
             send_rows(s, c, 0, 0, pieces * piece_rows)
 
@@ -382,14 +412,19 @@
             backs[c, m].start()
         moment[c, part_of(spot), :] = plane_out[c, spot]
 
-    for c in range(channels):
-        own_block(c)
-        if c > 0:
-            carry(c - 1)
-    carry(channels - 1)
-
-    for copy in backs.values():
-        copy.wait()
+    for group in (range(early), range(early, channels)):
+        for c in group:
+            own_block(c)
+        for c in group:
+            carry(c)
+        if group and group[0] == 0 and early:
+            for (c, m), copy in backs.items():
+                copy.wait()
+            invert(moment, 0, early, work, done, low21, early_high, early_low)
+
+    for (c, m), copy in backs.items():
+        if c >= early:
+            copy.wait()
     for copy in spreads.values():
         copy.wait_send()
     for copy in turns.values():
@@ -406,7 +441,7 @@
             tail.wait_send()
 
 
-def turned_and_carried(volts, coef, retain, inverse_weight, taps):
+def turned_and_carried(volts, coef, retain, inverse_weight, taps, early):
     inputs, antennas, frames = volts.shape
     channels = retain.shape[0]
     chan_count, tm_count = lax.axis_size("chan"), lax.axis_size("tm")
@@ -423,10 +458,12 @@
         rounds += 1
     chain_shape = (channels, rounds, PLANE - 1)
     return pl.pallas_call(
-        functools.partial(turn_kernel, taps, chan_count, tm_count),
+        functools.partial(turn_kernel, taps, chan_count, tm_count, early),
         out_shape=(
             jax.ShapeDtypeStruct((channels, columns, frames), jnp.bfloat16),
             jax.ShapeDtypeStruct((channels, 3 * half, half), jnp.float32),
+            jax.ShapeDtypeStruct((max(early, 1), columns, columns), jnp.bfloat16),
+            jax.ShapeDtypeStruct((max(early, 1), columns, columns), jnp.bfloat16),
         ),
         in_specs=[
             pl.BlockSpec(memory_space=pltpu.HBM),
@@ -434,8 +471,8 @@
             pl.BlockSpec(memory_space=pltpu.SMEM),
             pl.BlockSpec(memory_space=pltpu.SMEM),
         ],
-        out_specs=(pl.BlockSpec(memory_space=pltpu.VMEM), pl.BlockSpec(memory_space=pltpu.VMEM)),
-        scratch_shapes=[
+        out_specs=(pl.BlockSpec(memory_space=pltpu.VMEM),) * 4,
+        scratch_shapes=invert_scratch(early) + [
             pltpu.VMEM((inputs, antennas, HALO + frames), jnp.bfloat16),
             pltpu.VMEM((rows, taps * inputs * PIECE), jnp.bfloat16),
             pltpu.VMEM((chan_count - 1, channels, 2 * antennas, frames), jnp.bfloat16),
@@ -478,8 +515,11 @@
     powers = jnp.exp(rate[:, None] * ages.astype(jnp.float32))
     weight = frames * jnp.sum(powers[:, None, :] * held[None], -1)
     volts = voltages.reshape(branches * parts, antennas, frames)
-    spectra, moment = turned_and_carried(volts, coef, jnp.exp(rate), 1.0 / weight, taps)
-    return whitened_by(moment.reshape(channels, 3, BASE, BASE), spectra)
+    early = channels // 2
+    spectra, moment, high, low = turned_and_carried(
+        volts, coef, jnp.exp(rate), 1.0 / weight, taps, early
+    )
+    return whitened_by(moment, spectra, high, low, early)
 
 
 def solution(mesh):

time: 102 us -> 97.3 us (0.954)
  Pallas kernels: 96.7 us -> 92.3 us
    pallas_call x2, Pallas kernels: 96.7 us -> 92.3 us  [the longest x1 77 us: turned_and_carried(): pl.pallas_call(functools.partial(turn_kernel, taps, chan_count, tm_count,...]
where the time goes in v4:
time: 97.3 us; the launch traced here: 97.1 us
  Pallas kernels  92.3 us (95%)
  local copies, waits for them, and re-layouts  3.07 us (3%)
  other arithmetic  1.55 us (2%)
    pallas_call x1, Pallas kernels, turned_and_carried(): pl.pallas_call(functools.partial(turn_kernel, taps, chan_count, tm_count,...  77 us
    pallas_call x1, Pallas kernels, whitened_by(): pl.pallas_call(functools.partial(whiten_kernel, early), out_shape=jax.Sha...  15.3 us
    unnamed x2, local copies, waits for them, and re-layouts  2.19 us

profile of v4, /device:TPU:25, one launch (start us, length us, event | category | flops | bytes accessed | tf_op | source)
XLA Modules:
  0.0 97.1 jit_solution(8174020838189422042)
XLA Ops:
  0.0 0.7 negate_multiply_fusion
  0.7 0.1 multiply_exponential_fusion
  0.7 0.1 multiply_reduce_fusion
  0.8 0.7 broadcast_in_dim.10
  1.6 0.1 mul.47
  1.7 0.7 multiply_convert_fusion.coef
  2.4 0.0 copy-start
  2.4 2.2 %copy-done = bf16[8,2,64,2048]{3,2,1,0:T(8,128)(2,1)S(1)} copy-done((bf16[8,2,64,2048]{3,2,1,0:T(8,128)(2,1)S(1)}, bf16[8,2,64,2048]{3,2,1,0:T(8,128)(2,1)}, u32[]{:S(2)}) %copy-start) | copy-done | bytes 4194328
  4.6 77.0 %turn.1 = (bf16[4,256,2048]{2,1,0:T(8,128)(2,1)S(1)}, f32[4,384,128]{2,1,0:T(8,128)S(1)}, bf16[2,256,256]{2,1,0:T(8,128)(2,1)S(1)}, bf16[2,256,256]{2,1,0:T(8,128)(2,1)S(1)}) custom-call(bf16[16,64,2048]{2,1,0:T(8,128)(2,1)S(1)} %bitcast.1, bf16[16,128]{1,0:T(8,128)(2,1)S(1)} %multiply_convert_fusion.coef, f32[4]{0:T(128)S(1)} %get-tuple-element.14.retain, ...), custom_call_target="tpu_custom_call" | custom-call | tf_op jit(solution)/shard_map/turn/pallas_call | solution.py:460
  81.6 15.3 %whiten.1 = bf16[4,256,2048]{2,1,0:T(8,128)(2,1)} custom-call(f32[4,384,128]{2,1,0:T(8,128)S(1)} %get-tuple-element.9.moment, bf16[4,256,2048]{2,1,0:T(8,128)(2,1)S(1)} %get-tuple-element.10.x_ref, bf16[2,256,256]{2,1,0:T(8,128)(2,1)S(1)} %get-tuple-element.11.early_high, bf16[2,256,256]{2,1,0:T(8,128)(2,1)S(1)} %get-tuple-element.12.early_low), custom_call_target="tpu_custom_call" | custom-call | tf_op jit(solution)/shard_map/whiten/pallas_call | solution.py:162
  (3 shorter events, 0.0 us)
Async XLA Ops:
  2.4 2.2 %copy-start = (bf16[8,2,64,2048]{3,2,1,0:T(8,128)(2,1)S(1)}, bf16[8,2,64,2048]{3,2,1,0:T(8,128)(2,1)}, u32[]{:S(2)}) copy-start(bf16[8,2,64,2048]{3,2,1,0:T(8,128)(2,1)} %param.4) | copy-start | bytes 12582916

commit v5 on v4

--- a/solution.py
+++ b/solution.py
@@ -93,7 +93,7 @@
     lax.fori_loop(0, BASE // GROUP, group_step, 0)
 
 
-def invert(moment, first, count, work, done, low21, high, low, beside=(None, None)):
+def invert(moment, first, count, work, done, low21, high, low, beside=(None, None), between=None):
     def block(i, at):
         return moment[first + i, at * BASE : (at + 1) * BASE]
 
@@ -113,6 +113,8 @@
         low21[i] = exact_dot(factor, inverse, ((1,), (0,)))
         store(i, 0, 0, inverse)
         store(i, 0, BASE, jnp.zeros_like(inverse))
+    if between is not None:
+        between()
     eliminate(work, done, range(count), beside[1])
     for i in range(count):
         inverse = done[i]
@@ -362,35 +364,41 @@
             spreads[c, m].start()
         plane_in[c, spot] = gram[c, part_of(spot), :]
 
-    def carry(c):
+    def pass_on(c):
         for m in range(1, PLANE):
             spreads[c, m].wait_recv()
         keep = retain[c]
         total = plane_in[c, 0]
         for i in range(1, PLANE):
             total = total * keep + plane_in[c, i]
+        send_total(c, 0, total)
+
+    def send_total(c, r, total):
+        chain_out[c, r] = total
+        span = PLANE**r
+        for d in range(1, PLANE):
+            copy = remote(
+                chain_out.at[c, r], chain_in.at[c, r, d - 1],
+                chain_send.at[c, r, d - 1], chain_recv.at[c, r, d - 1],
+                chan, tm + PLANE * span * d,
+            )
+            chains[c, r, d] = copy
+
+            @pl.when(plane + span * d < plane_count)
+            def _():
+                copy.start()
+
+            @pl.when(plane < span * d)
+            def _():
+                chain_in[c, r, d - 1] = jnp.zeros_like(total)
+
+    def carry(c):
+        keep = retain[c]
         reach = keep * keep
         reach = reach * reach
         for r in range(rounds):
-            chain_out[c, r] = total
             span = PLANE**r
-            for d in range(1, PLANE):
-                copy = remote(
-                    chain_out.at[c, r], chain_in.at[c, r, d - 1],
-                    chain_send.at[c, r, d - 1], chain_recv.at[c, r, d - 1],
-                    chan, tm + PLANE * span * d,
-                )
-                chains[c, r, d] = copy
-
-                @pl.when(plane + span * d < plane_count)
-                def _():
-                    copy.start()
-
-                @pl.when(plane < span * d)
-                def _():
-                    chain_in[c, r, d - 1] = jnp.zeros_like(total)
-
-            earlier = jnp.zeros_like(total)
+            earlier = jnp.zeros(chain_out.shape[2:], jnp.float32)
             for d in range(PLANE - 1, 0, -1):
                 @pl.when(plane >= span * d)
                 def _():
@@ -398,7 +406,8 @@
 
                 earlier = earlier * reach + chain_in[c, r, d - 1]
             running = earlier if r == 0 else running + offset * earlier
-            total = total + reach * earlier
+            if r + 1 < rounds:
+                send_total(c, r + 1, chain_out[c, r] + reach * earlier)
             offset = reach**3 if r == 0 else offset * reach**3
             reach = reach**4
         for i in range(PLANE):
@@ -412,15 +421,31 @@
             backs[c, m].start()
         moment[c, part_of(spot), :] = plane_out[c, spot]
 
-    for group in (range(early), range(early, channels)):
-        for c in group:
+    def early_part():
+        for c in range(early):
             own_block(c)
-        for c in group:
+        for c in range(early):
+            pass_on(c)
+        for c in range(early):
             carry(c)
-        if group and group[0] == 0 and early:
-            for (c, m), copy in backs.items():
-                copy.wait()
-            invert(moment, 0, early, work, done, low21, early_high, early_low)
+        for copy in backs.values():
+            copy.wait()
+
+    if early:
+        early_part()
+        invert(
+            moment, 0, early, work, done, low21, early_high, early_low,
+            between=lambda: own_block(early),
+        )
+    else:
+        own_block(0)
+    pass_on(early)
+    for c in range(early, channels):
+        if c + 1 < channels:
+            own_block(c + 1)
+        carry(c)
+        if c + 1 < channels:
+            pass_on(c + 1)
 
     for (c, m), copy in backs.items():
         if c >= early:
@@ -486,7 +511,7 @@
             dma(plane_shape), dma(plane_shape),
         ],
         compiler_params=pltpu.CompilerParams(
-            collective_id=0, has_side_effects=True, vmem_limit_bytes=40 << 20
+            collective_id=0, has_side_effects=True, vmem_limit_bytes=47 << 20
         ),
         name="turn",
     )(volts, coef, retain, inverse_weight)

time: 97.3 us -> 92.4 us (0.950)
  Pallas kernels: 92.3 us -> 89.6 us
  local copies, waits for them, and re-layouts: 3.07 us -> 0.88 us
    pallas_call x1, Pallas kernels: 77 us -> 74.3 us  [turned_and_carried(): pl.pallas_call(functools.partial(turn_kernel, taps, chan_count, tm_count,...]
    unnamed x2 -> x0, local copies, waits for them, and re-layouts: 2.19 us -> none
where the time goes in v5:
time: 92.4 us; the launch traced here: 92.2 us
  Pallas kernels  89.6 us (97%)
  other arithmetic  1.55 us (2%)
    pallas_call x1, Pallas kernels, turned_and_carried(): pl.pallas_call(functools.partial(turn_kernel, taps, chan_count, tm_count,...  74.3 us
    pallas_call x1, Pallas kernels, whitened_by(): pl.pallas_call(functools.partial(whiten_kernel, early), out_shape=jax.Sha...  15.3 us

profile of v5, /device:TPU:25, one launch (start us, length us, event | category | flops | bytes accessed | tf_op | source)
XLA Modules:
  0.0 92.2 jit_solution(12852315173492011936)
XLA Ops:
  0.0 0.7 negate_multiply_fusion
  0.7 0.1 multiply_exponential_fusion
  0.7 0.1 multiply_reduce_fusion
  0.8 0.7 broadcast_in_dim.10
  1.6 0.1 mul.47
  1.7 0.7 multiply_convert_fusion.coef
  2.4 74.3 %turn.1 = (bf16[4,256,2048]{2,1,0:T(8,128)(2,1)S(1)}, f32[4,384,128]{2,1,0:T(8,128)S(1)}, bf16[2,256,256]{2,1,0:T(8,128)(2,1)S(1)}, bf16[2,256,256]{2,1,0:T(8,128)(2,1)S(1)}) custom-call(bf16[16,64,2048]{2,1,0:T(8,128)(2,1)} %bitcast.1, bf16[16,128]{1,0:T(8,128)(2,1)S(1)} %multiply_convert_fusion.coef, f32[4]{0:T(128)S(1)} %get-tuple-element.14.retain, ...), custom_call_target="tpu_custom_call" | custom-call | tf_op jit(solution)/shard_map/turn/pallas_call | solution.py:485
  76.7 15.3 %whiten.1 = bf16[4,256,2048]{2,1,0:T(8,128)(2,1)} custom-call(f32[4,384,128]{2,1,0:T(8,128)S(1)} %get-tuple-element.9.moment, bf16[4,256,2048]{2,1,0:T(8,128)(2,1)S(1)} %get-tuple-element.10.x_ref, bf16[2,256,256]{2,1,0:T(8,128)(2,1)S(1)} %get-tuple-element.11.early_high, bf16[2,256,256]{2,1,0:T(8,128)(2,1)S(1)} %get-tuple-element.12.early_low), custom_call_target="tpu_custom_call" | custom-call | tf_op jit(solution)/shard_map/whiten/pallas_call | solution.py:164
  (3 shorter events, 0.0 us)

commit v6 on v5

--- a/solution.py
+++ b/solution.py
@@ -57,7 +57,7 @@
             for i in range(len(channels)):
                 column = columns[i]
                 pivot = jnp.broadcast_to(column[p][at][inner : inner + 1, :], (SUB, BASE))
-                inverse = 1.0 / pivot
+                inverse = pl.reciprocal(pivot)
                 scales[i][at] = jnp.where(below == inner, inverse, scales[i][at])
                 for h in range(at, subs):
                     factor = column[p][h]
@@ -147,8 +147,11 @@
 
     copies = [pltpu.make_async_copy(result.at[c], out_ref.at[c], sems.at[c]) for c in range(channels)]
     beside = [tile_of(c) if c < early else None for c in range(2)]
-    invert(moment, early, channels - early, work, done, low21, high, low, beside)
-    for c in range(early):
+    invert(
+        moment, early, channels - early, work, done, low21, high, low, beside,
+        between=copies[0].start if early else None,
+    )
+    for c in range(1, early):
         copies[c].start()
     for c in range(early, channels):
         apply(c, high[c - early], low[c - early], slice(None))
@@ -282,16 +285,17 @@
 
     tiles = frames // TILE
     base = chan * (2 * antennas)
-    turns = {}
-
-    def send_rows(s, c, g, start, count):
-        turns[s, c, g] = remote(
-            outgoing.at[s - 1, c, pl.ds(start, count), :],
-            spectra.at[c, pl.ds(pl.multiple_of(base + start, piece_rows), count), :],
-            turn_send.at[s - 1, c, g], turn_recv.at[s - 1, c, g],
+    pairs = tiles // 2
+    turns = []
+
+    def turn_copy(s, c, slot, start, count, first, width):
+        lanes = pl.ds(first, width)
+        return remote(
+            outgoing.at[s - 1, c, pl.ds(start, count), lanes],
+            spectra.at[c, pl.ds(pl.multiple_of(base + start, piece_rows), count), lanes],
+            turn_send.at[s - 1, c, slot], turn_recv.at[s - 1, c, slot],
             (chan + s) % chan_count, tm,
         )
-        turns[s, c, g].start()
 
     for g in range(pieces):
         loads[g].wait()
@@ -319,25 +323,35 @@
                         outgoing[s - 1, c, g * piece_rows : (g + 1) * piece_rows, pl.ds(first, TILE)] = part
 
         def pair(step, _):
-            @pl.when((step == tiles // 2 - 1) & (tm > 0))
+            @pl.when((step == pairs - 1) & (tm > 0))
             def _():
                 tails[g].wait_recv()
 
-            places = [
-                pl.multiple_of(((step * 2 + u + 1) % tiles) * TILE, TILE) for u in range(2)
-            ]
+            start = pl.multiple_of((pairs - 1 - step) * (2 * TILE), 2 * TILE)
+            places = [pl.multiple_of(start + u * TILE, TILE) for u in range(2)]
             results = [tile(first) for first in places]
             for first, result in zip(places, results):
                 store(first, result)
+            for c in range(max(early, 1)):
+                for s in range(1, chan_count):
+                    turn_copy(
+                        s, c, g * pairs + step, g * piece_rows, piece_rows, start, 2 * TILE
+                    ).start()
             return 0
 
-        lax.fori_loop(0, tiles // 2, pair, 0)
+        lax.fori_loop(0, pairs, pair, 0)
         for c in range(max(early, 1)):
             for s in range(1, chan_count):
-                send_rows(s, c, g, g * piece_rows, piece_rows)
+                for step in range(pairs):
+                    first = (pairs - 1 - step) * (2 * TILE)
+                    slot = g * pairs + step
+                    turns.append(
+                        (c, turn_copy(s, c, slot, g * piece_rows, piece_rows, first, 2 * TILE))
+                    )
     for c in range(max(early, 1), channels):
         for s in range(1, chan_count):
-            send_rows(s, c, 0, 0, pieces * piece_rows)
+            turns.append((c, turn_copy(s, c, 0, 0, pieces * piece_rows, 0, frames)))
+            turns[-1][1].start()
 
     spreads, chains, backs = {}, {}, {}
     half = 2 * antennas * chan_count // 2
@@ -346,8 +360,8 @@
         return pl.ds(pl.multiple_of(index * quarter, 8), quarter)
 
     def own_block(c):
-        for key, copy in turns.items():
-            if key[1] == c:
+        for owner, copy in turns:
+            if owner == c:
                 copy.wait_recv()
         x = spectra[c]
         product = lax.dot_general(
@@ -452,7 +466,7 @@
             copy.wait()
     for copy in spreads.values():
         copy.wait_send()
-    for copy in turns.values():
+    for _, copy in turns:
         copy.wait_send()
 
     for (c, r, d), copy in chains.items():
@@ -476,7 +490,7 @@
     rows = coef.shape[0] * PIECE
     pieces = antennas // PIECE
     dma = pltpu.SemaphoreType.DMA
-    turn_shape = (chan_count - 1, channels, pieces)
+    turn_shape = (chan_count - 1, channels, pieces * (frames // (2 * TILE)))
     plane_shape = (channels, PLANE - 1)
     rounds = 1
     while PLANE ** (rounds + 1) < tm_count:

time: 92.4 us -> 90.9 us (0.984)
  Pallas kernels: 89.6 us -> 88.1 us
    pallas_call x1, Pallas kernels: 74.3 us -> 72.8 us  [turned_and_carried(): pl.pallas_call(functools.partial(turn_kernel, taps, chan_count, tm_count,...]
where the time goes in v6:
time: 90.9 us; the launch traced here: 90.7 us
  Pallas kernels  88.1 us (97%)
  other arithmetic  1.55 us (2%)
    pallas_call x1, Pallas kernels, turned_and_carried(): pl.pallas_call(functools.partial(turn_kernel, taps, chan_count, tm_count,...  72.8 us
    pallas_call x1, Pallas kernels, whitened_by(): pl.pallas_call(functools.partial(whiten_kernel, early), out_shape=jax.Sha...  15.3 us

profile of v6, /device:TPU:25, one launch (start us, length us, event | category | flops | bytes accessed | tf_op | source)
XLA Modules:
  0.0 90.7 jit_solution(11432596954715099178)
XLA Ops:
  0.0 0.7 negate_multiply_fusion
  0.7 0.1 multiply_exponential_fusion
  0.7 0.1 multiply_reduce_fusion
  0.8 0.7 broadcast_in_dim.10
  1.6 0.1 mul.47
  1.7 0.7 multiply_convert_fusion.coef
  2.4 72.8 %turn.1 = (bf16[4,256,2048]{2,1,0:T(8,128)(2,1)S(1)}, f32[4,384,128]{2,1,0:T(8,128)S(1)}, bf16[2,256,256]{2,1,0:T(8,128)(2,1)S(1)}, bf16[2,256,256]{2,1,0:T(8,128)(2,1)S(1)}) custom-call(bf16[16,64,2048]{2,1,0:T(8,128)(2,1)} %bitcast.1, bf16[16,128]{1,0:T(8,128)(2,1)S(1)} %multiply_convert_fusion.coef, f32[4]{0:T(128)S(1)} %get-tuple-element.14.retain, ...), custom_call_target="tpu_custom_call" | custom-call | tf_op jit(solution)/shard_map/turn/pallas_call | solution.py:499
  75.2 15.3 %whiten.1 = bf16[4,256,2048]{2,1,0:T(8,128)(2,1)} custom-call(f32[4,384,128]{2,1,0:T(8,128)S(1)} %get-tuple-element.9.moment, bf16[4,256,2048]{2,1,0:T(8,128)(2,1)S(1)} %get-tuple-element.10.x_ref, bf16[2,256,256]{2,1,0:T(8,128)(2,1)S(1)} %get-tuple-element.11.early_high, bf16[2,256,256]{2,1,0:T(8,128)(2,1)S(1)} %get-tuple-element.12.early_low), custom_call_target="tpu_custom_call" | custom-call | tf_op jit(solution)/shard_map/whiten/pallas_call | solution.py:167
  (3 shorter events, 0.0 us)
